TPU v7x, 32 devices: a whole 2x2x4 slice. The times are simulated.
32 devices in a mesh: samp: 4 (over x, core), blk: 8 (over z, y).
Axes of the slice: x: 2, y: 2, z: 4, core: 2. Of those that a mesh axis runs over, the one named last changes fastest.
Arguments:
- inputs: bfloat16 [4, 1024, 1024], P('samp', 'blk'), may hold values from -6 to 6
- cot_first: bfloat16 [4, 1024, 1024], P('samp', 'blk'), may hold values from -6 to 6
- cot_second: bfloat16 [4, 1024, 1024], P('samp', 'blk'), may hold values from -6 to 6
- valid_flags: int32 [4, 1024], P('samp', 'blk'), may hold values from 0 to 1, as said below
- lead_steps: int32 [2, 4], P(None, 'samp'), may hold values from 0 to 7
- masters: float32 [192, 256, 256], P('blk'), may hold values from -4 to 4
- assignment: int32 [192], replicated, may hold values from 0 to 191, as said below
- left_start: float32 [192, 256], P('blk'), may hold values from 256 to 1024
- right_start: float32 [192, 256], P('blk'), may hold values from 256 to 1024
- vectors: float32 [20, 1024], replicated, may hold values from -1.6 to 1.6
- vec_moment: float32 [20, 1024], replicated, may hold values from 0.5 to 8
Outputs:
- pred_first: bfloat16 [4, 1024, 1024], P('samp', 'blk')
- pred_second: bfloat16 [4, 1024, 1024], P('samp', 'blk')
- input_grad: float32 [4, 1024, 1024], P('samp', 'blk')
- matrix_grads: float32 [192, 256, 256], P('blk')
- left_stats: float32 [192, 256, 256], P('blk')
- right_stats: float32 [192, 256, 256], P('blk')
- new_masters: float32 [192, 256, 256], P('blk')
- new_copies: bfloat16 [192, 256, 256], P('blk')
- vec_grads: float32 [20, 1024], replicated
- vec_moments: float32 [20, 1024], replicated
- new_vectors: float32 [20, 1024], replicated
Inputs may be any that keep to these rules, and one draw needn't show every extreme that they name: `valid_flags`: 1 where a patch has data; the first and the last patch of every sample are 1. `assignment`: a permutation of 0 to 191; slots are dealt to the devices of blk in order, 24 each.
All inputs are finite; a program needn't handle non-finite values.
Results may differ from a plain program's by a relative error of at most 0.02.
Values may be sent and summed in bfloat16 or wider, within the bound.
A program may use at most 320 MiB of HBM per device.

v0:
```python
import math

import jax
import jax.numpy as jnp
from jax import lax
from jax.sharding import PartitionSpec as P

D = 1024
HEADS = 16
FF = 4096
HD = 64
LEADS = 8
BS = 256
ITERS = 6
NB = 192


HIGH = lax.Precision.HIGHEST
step_rate = 0.5
vector_rate = 0.3
masked = 1000000000.0


def assemble(blocks, height, breadth):
    return (
        blocks.reshape(height // BS, breadth // BS, BS, BS)
        .transpose(0, 2, 1, 3)
        .reshape(height, breadth)
    )


def carve(matrix):
    height, breadth = matrix.shape
    return (
        matrix.reshape(height // BS, BS, breadth // BS, BS)
        .transpose(0, 2, 1, 3)
        .reshape(-1, BS, BS)
    )


def unpack(blocks):
    first_end = 3 * D * D // (BS * BS)
    second_end = first_end + D * D // (BS * BS)
    third_end = second_end + D * FF // (BS * BS)
    qkv_weight = assemble(blocks[:first_end], D, 3 * D)
    out_weight = assemble(blocks[first_end:second_end], D, D)
    up_weight = assemble(blocks[second_end:third_end], D, FF)
    down_weight = assemble(blocks[third_end:], FF, D)
    return (qkv_weight, out_weight, up_weight, down_weight)


def norm_layer(value, gain, shift):
    centred = value - jnp.mean(value, axis=-1, keepdims=True)
    spread = jnp.mean(centred * centred, axis=-1, keepdims=True)
    return centred * lax.rsqrt(spread + 1e-06) * gain + shift


def gelu_exact(value):
    return jax.nn.gelu(value, approximate=False)


def heads_of(tensor):
    return tensor.reshape(tensor.shape[0], tensor.shape[1], HEADS, HD)


def split_rows(member, count, width):
    shaped = member.reshape((member.shape[0], count, width) + member.shape[2:])
    return jnp.moveaxis(shaped, 1, 0)


def in_blocks(update, carry, members, length):
    width = math.gcd(length, 1024)
    count = length // width
    if count == 1:
        return update(carry, members, 0)
    stacked = tuple([split_rows(member, count, width) for member in members])
    offsets = jnp.arange(count, dtype=jnp.int32) * width

    def advance(state, item):
        return (update(state, item[0], item[1]), None)

    result, unused = lax.scan(advance, carry, (stacked, offsets))
    return result


def forward_update(query_heads, scaling):

    def update(carry, members, offset):
        running_max, running_sum, weighted = carry
        key_part, value_part, flag_part = members
        bias = (flag_part.astype(jnp.float32) - 1.0) * masked
        scores = (
            jnp.einsum(
                "sqhd,skhd->shqk",
                query_heads,
                heads_of(key_part),
                preferred_element_type=jnp.float32,
            )
            * scaling
            + bias[:, None, None, :]
        )
        new_max = jnp.maximum(running_max, jnp.max(scores, axis=-1))
        shrink = jnp.exp(running_max - new_max)
        expos = jnp.exp(scores - new_max[..., None])
        running_sum = running_sum * shrink + jnp.sum(expos, axis=-1)
        weighted = weighted * shrink[..., None] + jnp.einsum(
            "shqk,skhd->shqd",
            expos.astype(jnp.bfloat16),
            heads_of(value_part),
            preferred_element_type=jnp.float32,
        )
        return (new_max, running_sum, weighted)

    return update


def query_grad_update(query_heads, dout_heads, log_total, inner, scaling):

    def update(carry, members, offset):
        key_part, value_part, flag_part = members
        bias = (flag_part.astype(jnp.float32) - 1.0) * masked
        scores = (
            jnp.einsum(
                "sqhd,skhd->shqk",
                query_heads,
                heads_of(key_part),
                preferred_element_type=jnp.float32,
            )
            * scaling
            + bias[:, None, None, :]
        )
        probs = jnp.exp(scores - log_total[..., None])
        dprobs = jnp.einsum(
            "sqhd,skhd->shqk", dout_heads, heads_of(value_part), preferred_element_type=jnp.float32
        )
        dscores = (probs * (dprobs - inner[..., None])).astype(jnp.bfloat16)
        return (
            carry
            + jnp.einsum(
                "shqk,skhd->sqhd", dscores, heads_of(key_part), preferred_element_type=jnp.float32
            )
            * scaling
        )

    return update


def key_grad_update(key_heads, value_heads, key_bias, total_rows, inner_rows, scaling, anchor):

    def update(carry, members, offset):
        grad_keys, grad_values = carry
        query_part, dout_part = members
        length = query_part.shape[1]
        total_part = jnp.transpose(
            lax.dynamic_slice_in_dim(total_rows, anchor + offset, length, 1), (0, 2, 1)
        )
        inner_part = jnp.transpose(
            lax.dynamic_slice_in_dim(inner_rows, anchor + offset, length, 1), (0, 2, 1)
        )
        query_heads = heads_of(query_part)
        dout_heads = heads_of(dout_part)
        scores = (
            jnp.einsum(
                "sqhd,skhd->shqk", query_heads, key_heads, preferred_element_type=jnp.float32
            )
            * scaling
            + key_bias[:, None, None, :]
        )
        probs = jnp.exp(scores - total_part[..., None])
        dprobs = jnp.einsum(
            "sqhd,skhd->shqk", dout_heads, value_heads, preferred_element_type=jnp.float32
        )
        dscores = (probs * (dprobs - inner_part[..., None])).astype(jnp.bfloat16)
        grad_values = grad_values + jnp.einsum(
            "shqk,sqhd->skhd",
            probs.astype(jnp.bfloat16),
            dout_heads,
            preferred_element_type=jnp.float32,
        )
        grad_keys = (
            grad_keys
            + jnp.einsum(
                "shqk,sqhd->skhd", dscores, query_heads, preferred_element_type=jnp.float32
            )
            * scaling
        )
        return (grad_keys, grad_values)

    return update


def invert_root(stat):
    identity = jnp.eye(stat.shape[0], dtype=jnp.float32)
    frobenius = jnp.sqrt(jnp.sum(stat * stat))
    approx = identity * lax.rsqrt(jnp.sqrt(frobenius))
    moving = stat / frobenius
    for iteration in range(ITERS):
        factor = (5.0 * identity - moving) * 0.25
        approx = jnp.dot(approx, factor, precision=HIGH)
        square = jnp.dot(factor, factor, precision=HIGH)
        moving = jnp.dot(jnp.dot(square, square, precision=HIGH), moving, precision=HIGH)
    return approx


def precondition(gradient, left_diag, right_diag, weight):
    scaled = gradient * lax.rsqrt(jnp.mean(gradient * gradient) + 1e-06)
    identity = jnp.eye(BS, dtype=jnp.float32)
    left_new = 0.5 * identity * left_diag[None, :] + 0.5 * jnp.dot(scaled, scaled.T, precision=HIGH)
    right_new = 0.5 * identity * right_diag[None, :] + 0.5 * jnp.dot(
        scaled.T, scaled, precision=HIGH
    )
    direction = jnp.dot(
        jnp.dot(invert_root(left_new), scaled, precision=HIGH),
        invert_root(right_new),
        precision=HIGH,
    )
    ratio = jnp.sqrt(jnp.mean(weight * weight)) * lax.rsqrt(jnp.mean(direction * direction) + 1e-06)
    return (left_new, right_new, weight - step_rate * ratio * direction)


def local(
    inputs,
    cot_first,
    cot_second,
    valid_flags,
    lead_steps,
    masters,
    assignment,
    left_start,
    right_start,
    vectors,
    vec_moment,
):
    copies = lax.all_gather(masters.astype(jnp.bfloat16), "blk", axis=0, tiled=True)
    blocks = jnp.take(copies, assignment, axis=0)
    qkv_weight, out_weight, up_weight, down_weight = unpack(blocks)
    scaling = HD ** (-0.5)
    flags_low = valid_flags.astype(jnp.bfloat16)
    key_bias = (valid_flags.astype(jnp.float32) - 1.0) * masked
    lead_base = 8 + FF // D
    lead_table = vectors[lead_base:]
    samples = inputs.shape[0]
    patches = inputs.shape[1]

    def forward(hidden_in, lead_ids):
        chosen = (lead_ids[:, None] == jnp.arange(LEADS, dtype=jnp.int32)[None, :]).astype(
            jnp.float32
        )
        lead_rows = jnp.dot(chosen, lead_table, precision=HIGH)
        hidden = hidden_in + lead_rows[:, None, :]
        normed_low = norm_layer(hidden, vectors[0], vectors[1]).astype(jnp.bfloat16)
        packed = jnp.einsum(
            "spd,de->spe", normed_low, qkv_weight, preferred_element_type=jnp.float32
        )
        queries = (packed[..., :D] + vectors[2]).astype(jnp.bfloat16)
        keys_low = packed[..., D : 2 * D].astype(jnp.bfloat16)
        values_low = (packed[..., 2 * D :] + vectors[3]).astype(jnp.bfloat16)
        start_state = (
            jnp.full((samples, HEADS, patches), -1e30, jnp.float32),
            jnp.zeros((samples, HEADS, patches), jnp.float32),
            jnp.zeros((samples, HEADS, patches, HD), jnp.float32),
        )
        update = forward_update(heads_of(queries), scaling)
        gathered = None
        piece = (
            lax.all_gather(keys_low, "blk", axis=1, tiled=True),
            lax.all_gather(values_low, "blk", axis=1, tiled=True),
            lax.all_gather(flags_low, "blk", axis=1, tiled=True),
        )
        running_max, running_sum, weighted = in_blocks(
            update, start_state, piece, piece[0].shape[1]
        )
        attended = jnp.transpose(weighted / running_sum[..., None], (0, 2, 1, 3)).reshape(
            samples, patches, D
        )
        log_total = running_max + jnp.log(running_sum)
        attended_low = attended.astype(jnp.bfloat16)
        middle = (
            hidden
            + jnp.einsum(
                "spd,de->spe", attended_low, out_weight, preferred_element_type=jnp.float32
            )
            + vectors[4]
        )
        normed_two = norm_layer(middle, vectors[5], vectors[6]).astype(jnp.bfloat16)
        upward = jnp.einsum(
            "spd,df->spf", normed_two, up_weight, preferred_element_type=jnp.float32
        ) + vectors[8:lead_base].reshape(FF)
        activated = gelu_exact(upward).astype(jnp.bfloat16)
        result = (
            middle
            + jnp.einsum("spf,fd->spd", activated, down_weight, preferred_element_type=jnp.float32)
            + vectors[7]
        )
        saved = (
            hidden,
            normed_low,
            queries,
            keys_low,
            values_low,
            attended,
            attended_low,
            log_total,
            middle,
            normed_two,
            upward,
            activated,
            chosen,
            gathered,
        )
        return (result, saved)

    def backward(grad_out, saved):
        (
            hidden,
            normed_low,
            queries,
            keys_low,
            values_low,
            attended,
            attended_low,
            log_total,
            middle,
            normed_two,
            upward,
            activated,
            chosen,
            gathered,
        ) = saved
        grad_two = grad_out.astype(jnp.bfloat16)
        down_grad = jnp.einsum(
            "spf,spd->fd", activated, grad_two, preferred_element_type=jnp.float32
        )
        down_bias = jnp.sum(grad_two.astype(jnp.float32), axis=(0, 1))
        grad_act = jnp.einsum(
            "spd,fd->spf", grad_two, down_weight, preferred_element_type=jnp.float32
        )
        gelu_value, gelu_pull = jax.vjp(gelu_exact, upward)
        grad_up = gelu_pull(grad_act)[0].astype(jnp.bfloat16)
        up_grad = jnp.einsum("spd,spf->df", normed_two, grad_up, preferred_element_type=jnp.float32)
        up_bias = jnp.sum(grad_up.astype(jnp.float32), axis=(0, 1))
        grad_normed_two = jnp.einsum(
            "spf,df->spd", grad_up, up_weight, preferred_element_type=jnp.float32
        )
        norm_value, norm_pull = jax.vjp(norm_layer, middle, vectors[5], vectors[6])
        grad_middle_norm, gain_two, shift_two = norm_pull(grad_normed_two)
        grad_middle = grad_out + grad_middle_norm
        grad_one = grad_middle.astype(jnp.bfloat16)
        out_grad = jnp.einsum(
            "spd,spe->de", attended_low, grad_one, preferred_element_type=jnp.float32
        )
        out_bias = jnp.sum(grad_one.astype(jnp.float32), axis=(0, 1))
        grad_attended = jnp.einsum(
            "spe,de->spd", grad_one, out_weight, preferred_element_type=jnp.float32
        ).astype(jnp.bfloat16)
        inner = jnp.sum(
            (grad_attended.astype(jnp.float32) * attended).reshape(samples, patches, HEADS, HD),
            axis=-1,
        )
        inner_heads = jnp.transpose(inner, (0, 2, 1))
        zero_query = jnp.zeros((samples, patches, HEADS, HD), jnp.float32)
        update_query = query_grad_update(
            heads_of(queries), heads_of(grad_attended), log_total, inner_heads, scaling
        )
        piece = (
            lax.all_gather(keys_low, "blk", axis=1, tiled=True),
            lax.all_gather(values_low, "blk", axis=1, tiled=True),
            lax.all_gather(flags_low, "blk", axis=1, tiled=True),
        )
        grad_query = in_blocks(update_query, zero_query, piece, piece[0].shape[1])
        total_rows, inner_rows = (
            lax.all_gather(jnp.transpose(log_total, (0, 2, 1)), "blk", axis=1, tiled=True),
            lax.all_gather(inner, "blk", axis=1, tiled=True),
        )
        key_heads = heads_of(keys_low)
        value_heads = heads_of(values_low)
        zero_pair = (zero_query, zero_query)
        piece = (
            lax.all_gather(queries, "blk", axis=1, tiled=True),
            lax.all_gather(grad_attended, "blk", axis=1, tiled=True),
        )
        update_keys = key_grad_update(
            key_heads, value_heads, key_bias, total_rows, inner_rows, scaling, jnp.int32(0)
        )
        grad_keys, grad_values = in_blocks(update_keys, zero_pair, piece, piece[0].shape[1])
        grad_packed = jnp.concatenate(
            [
                grad_query.reshape(samples, patches, D),
                grad_keys.reshape(samples, patches, D),
                grad_values.reshape(samples, patches, D),
            ],
            axis=-1,
        ).astype(jnp.bfloat16)
        qkv_grad = jnp.einsum(
            "spd,spe->de", normed_low, grad_packed, preferred_element_type=jnp.float32
        )
        query_bias = jnp.sum(grad_packed[..., :D].astype(jnp.float32), axis=(0, 1))
        value_bias = jnp.sum(grad_packed[..., 2 * D :].astype(jnp.float32), axis=(0, 1))
        grad_normed = jnp.einsum(
            "spe,de->spd", grad_packed, qkv_weight, preferred_element_type=jnp.float32
        )
        first_value, first_pull = jax.vjp(norm_layer, hidden, vectors[0], vectors[1])
        grad_hidden_norm, gain_one, shift_one = first_pull(grad_normed)
        grad_hidden = grad_middle + grad_hidden_norm
        lead_grad = jnp.dot(chosen.T, jnp.sum(grad_hidden, axis=1), precision=HIGH)
        vec_rows = jnp.concatenate(
            [
                gain_one[None],
                shift_one[None],
                query_bias[None],
                value_bias[None],
                out_bias[None],
                gain_two[None],
                shift_two[None],
                down_bias[None],
                up_bias.reshape(FF // D, D),
                lead_grad,
            ],
            axis=0,
        )
        return (grad_hidden, (qkv_grad, out_grad, up_grad, down_grad), vec_rows)

    earlier, saved_one = forward(inputs.astype(jnp.float32), lead_steps[0])
    later, saved_two = forward(earlier, lead_steps[1])
    grad_between, mats_two, vec_two = backward(cot_second.astype(jnp.float32), saved_two)
    input_grad, mats_one, vec_one = backward(
        cot_first.astype(jnp.float32) + grad_between, saved_one
    )
    grad_blocks = jnp.concatenate(
        [
            carve(mats_one[0] + mats_two[0]),
            carve(mats_one[1] + mats_two[1]),
            carve(mats_one[2] + mats_two[2]),
            carve(mats_one[3] + mats_two[3]),
        ],
        axis=0,
    )
    position = jnp.arange(NB, dtype=jnp.int32)
    inverse = jnp.sum(
        jnp.where(assignment[None, :] == position[:, None], position[None, :], 0), axis=1
    )
    slotted = jnp.take(grad_blocks, inverse, axis=0)
    shared = lax.psum_scatter(slotted, "blk", scatter_dimension=0, tiled=True)
    matrix_grads = lax.psum(shared.astype(jnp.bfloat16), "samp").astype(jnp.float32)
    vec_grads = lax.psum(vec_one + vec_two, ("samp", "blk"))
    left_stats, right_stats, new_masters = jax.vmap(precondition)(
        matrix_grads, left_start, right_start, masters
    )
    scaled_vec = vec_grads * lax.rsqrt(
        jnp.mean(vec_grads * vec_grads, axis=1, keepdims=True) + 1e-06
    )
    vec_moments = 0.5 * vec_moment + 0.5 * scaled_vec * scaled_vec
    new_vectors = vectors - vector_rate * scaled_vec * lax.rsqrt(vec_moments)
    return (
        earlier.astype(jnp.bfloat16),
        later.astype(jnp.bfloat16),
        input_grad,
        matrix_grads,
        left_stats,
        right_stats,
        new_masters,
        new_masters.astype(jnp.bfloat16),
        vec_grads,
        vec_moments,
        new_vectors,
    )


def solution(mesh):
    placed = (
        P("samp", "blk", None),
        P("samp", "blk", None),
        P("samp", "blk", None),
        P("samp", "blk"),
        P(None, "samp"),
        P("blk", None, None),
        P(),
        P("blk", None),
        P("blk", None),
        P(),
        P(),
    )
    return jax.shard_map(
        local,
        mesh=mesh,
        in_specs=placed,
        out_specs=(
            P("samp", "blk", None),
            P("samp", "blk", None),
            P("samp", "blk", None),
            P("blk", None, None),
            P("blk", None, None),
            P("blk", None, None),
            P("blk", None, None),
            P("blk", None, None),
            P(),
            P(),
            P(),
        ),
        check_vma=False,
    )
```

profile of v0, /device:TPU:3, one launch (start us, length us, event | category | flops | bytes accessed | tf_op | source)
XLA Modules:
  0.0 2767.5 jit_solution(15233168239775667870)
XLA Ops:
  17.5 479.4 %all-gather.14.cloned.1.call-done = bf16[192,256,256]{2,1,0:T(8,128)(2,1)} async-done(((bf16[24,256,256]{2,1,0:T(8,128)(2,1)}), bf16[192,256,256]{2,1,0:T(8,128)(2,1)}) %all-gather.14.cloned.1.call-update) | async-done | bytes 25165840 | tf_op jit(solution)/shard_map/all_gather | solution.py:234
  496.9 19.6 gather_fusion
  516.5 21.1 broadcast_select_fusion.1
  568.2 15.9 all_gather.51
  587.0 11.9 fusion.290
  610.4 12.3 copy.134
  622.7 15.0 copy.107
  637.7 12.3 copy.136
  694.7 44.5 %all-gather.20.cloned.1.call-done = bf16[1,1024,1024]{2,1,0:T(8,128)(2,1)} async-done(((bf16[1,128,1024]{2,1,0:T(8,128)(2,1)}), bf16[1,1024,1024]{2,1,0:T(8,128)(2,1)}) %all-gather.20.cloned.1.call-update) | async-done | bytes 2097168 | tf_op jit(solution)/shard_map/all_gather | solution.py:266
  750.2 38.8 %all-gather.22.cloned.1.call-done = bf16[1,1024,1024]{2,1,0:T(8,128)(2,1)} async-done(((bf16[1,128,1024]{2,1,0:T(8,128)(2,1)}), bf16[1,1024,1024]{2,1,0:T(8,128)(2,1)}) %all-gather.22.cloned.1.call-update) | async-done | bytes 2097168 | tf_op jit(solution)/shard_map/all_gather | solution.py:267
  842.8 26.3 all_gather.60
  893.1 24.2 all_gather.56
  918.3 26.3 all-gather.1
  1014.0 14.2 convolution_add_fusion
  1044.1 20.4 reshape.1305
  1064.5 14.4 copy.129
  1100.7 11.7 copy.128
  1112.5 24.4 all-gather.3
  1175.2 12.7 copy.125
  1187.9 15.7 reshape.1299
  1203.6 14.6 copy.126
  1218.1 34.4 %pad_maximum_fusion = f32[192,256,256]{2,1,0:T(8,128)} fusion(f32[64,256,256]{2,1,0:T(8,128)} %bitcast.458, f32[64,256,256]{2,1,0:T(8,128)} %bitcast.459, f32[16,256,256]{2,1,0:T(8,128)} %bitcast.482, f32[48,256,256]{2,1,0:T(8,128)} %bitcast.464), kind=kLoop, calls=%fused_computation.2 | loop fusion | flops 37748736 | bytes 100663296 | tf_op jit(solution)/shard_map/concatenate | solution.py:429
  1252.6 34.2 %gather_fusion.1 = f32[192,256,256]{2,1,0:T(8,128)} fusion(f32[192,256,256]{2,1,0:T(8,128)} %pad_maximum_fusion, s32[1024]{0:T(1024)} %pad_clamp_fusion), kind=kCustom, calls=%fused_computation.1 | custom fusion | bytes 100664064 | tf_op jit(solution)/shard_map/jit(_take)/gather | solution.py:442
  1286.8 34.4 %broadcast_select_fusion = f32[192,256,256]{2,1,0:T(8,128)} fusion(f32[192,256,256]{2,1,0:T(8,128)} %gather_fusion.1, pred[192]{0:T(512)(128)(4,1)S(1)} %copy-done.100), kind=kLoop, calls=%fused_computation.3 | loop fusion | flops 12582912 | bytes 100663488 | tf_op jit(solution)/shard_map/jit(_take)/select_n | solution.py:442
  1330.1 799.3 %reduce-scatter.2.cloned.1.call-done = f32[24,256,256]{2,1,0:T(8,128)} async-done(((f32[192,256,256]{2,1,0:T(8,128)}), f32[24,256,256]{2,1,0:T(8,128)}) %reduce-scatter.2.cloned.1.call-update) | async-done | bytes 6291472 | tf_op jit(solution)/shard_map/reduce_scatter | solution.py:443
  2145.2 110.7 %all-reduce.5.cloned.1.call-done = f32[20,1024]{1,0:T(8,128)} async-done(((f32[20,1024]{1,0:T(8,128)}), f32[20,1024]{1,0:T(8,128)}) %all-reduce.5.cloned.1.call-update) | async-done | bytes 81936 | tf_op jit(solution)/shard_map/psum | solution.py:445
  2258.6 69.0 %all-reduce.3.cloned.1.call-done = bf16[24,256,256]{2,1,0:T(8,128)(2,1)} async-done(((bf16[24,256,256]{2,1,0:T(8,128)(2,1)}), bf16[24,256,256]{2,1,0:T(8,128)(2,1)}) %all-reduce.3.cloned.1.call-update) | async-done | bytes 3145744 | tf_op jit(solution)/shard_map/psum | solution.py:444
  2351.6 13.9 fusion.16
  2365.5 14.3 fusion.14
  2406.3 12.8 fusion.279
  2558.1 14.5 fusion.11
  2730.9 14.4 fusion.6
  (492 shorter events, 723.5 us)
Async XLA Ops:
  7.2 489.7 %all-gather.14.cloned.1.call-start = ((), (), s32[]{:S(2)}) async-start(), calls=%async_computation.1 | async-start | bytes 28311552 | tf_op jit(solution)/shard_map/all_gather | solution.py:234
  15.1 635.2 %all-gather.16.cloned.1.call-start = ((), (), s32[]{:S(2)}) async-start(), calls=%async_computation.2 | async-start | bytes 2359296 | tf_op jit(solution)/shard_map/all_gather | solution.py:266
  16.5 659.4 %copy-start.53 = (f32[1,1024]{1,0:T(1,128)}, f32[1,1024]{1,0:T(1,128)S(1)}, u32[]{:S(2)}) copy-start(f32[1,1024]{1,0:T(1,128)S(1)} %fusion.207) | copy-start | bytes 12292
  16.7 542.5 %copy-start.65 = (f32[128]{0:T(128)}, f32[128]{0:T(128)S(1)}, u32[]{:S(2)}) copy-start(f32[128]{0:T(128)S(1)} %broadcast_multiply_fusion.5) | copy-start | bytes 1540
  17.5 541.7 %copy-start.71 = (f32[128]{0:T(128)}, f32[128]{0:T(128)S(1)}, u32[]{:S(2)}) copy-start(f32[128]{0:T(128)S(1)} %fusion.227) | copy-start | bytes 1540
  17.5 660.6 %copy-start.91 = (f32[1,1024]{1,0:T(1,128)}, f32[1,1024]{1,0:T(1,128)S(1)}, u32[]{:S(2)}) copy-start(f32[1,1024]{1,0:T(1,128)S(1)} %get-tuple-element.58) | copy-start | bytes 12292
  17.5 669.5 %copy-start.55 = (f32[1,1024]{1,0:T(1,128)}, f32[1,1024]{1,0:T(1,128)S(1)}, u32[]{:S(2)}) copy-start(f32[1,1024]{1,0:T(1,128)S(1)} %get-tuple-element.56) | copy-start | bytes 12292
  566.0 98.9 %all-gather.18.cloned.1.call-start = ((), (), s32[]{:S(2)}) async-start(), calls=%async_computation.3 | async-start | bytes 2359296 | tf_op jit(solution)/shard_map/all_gather | solution.py:267
  568.1 82.0 %copy-start.32 = (bf16[1,128,1024]{2,1,0:T(8,128)(2,1)}, bf16[1,128,1024]{2,1,0:T(8,128)(2,1)S(1)}, u32[]{:S(2)}) copy-start(bf16[1,128,1024]{2,1,0:T(8,128)(2,1)S(1)} %get-tuple-element.47) | copy-start | bytes 786436
  568.1 171.1 %all-gather.20.cloned.1.call-start = ((), (), s32[]{:S(2)}) async-start(), calls=%async_computation.4 | async-start | bytes 2359296 | tf_op jit(solution)/shard_map/all_gather | solution.py:266
  584.8 401.1 %copy-start.57 = (f32[1,1024]{1,0:T(1,128)}, f32[1,1024]{1,0:T(1,128)S(1)}, u32[]{:S(2)}) copy-start(f32[1,1024]{1,0:T(1,128)S(1)} %fusion.205) | copy-start | bytes 12292
  686.8 299.1 %copy-start.6 = (f32[1,128,1024]{2,1,0:T(8,128)}, f32[1,128,1024]{2,1,0:T(8,128)S(1)}, u32[]{:S(2)}) copy-start(f32[1,128,1024]{2,1,0:T(8,128)S(1)} %get-tuple-element.78) | copy-start | bytes 1572868
  686.8 299.1 %copy-start.69 = (f32[128]{0:T(128)}, f32[128]{0:T(128)S(1)}, u32[]{:S(2)}) copy-start(f32[128]{0:T(128)S(1)} %broadcast_multiply_fusion.3) | copy-start | bytes 1540
  687.1 298.9 %copy-start.83 = (f32[128]{0:T(128)}, f32[128]{0:T(128)S(1)}, u32[]{:S(2)}) copy-start(f32[128]{0:T(128)S(1)} %fusion.229) | copy-start | bytes 1540
  691.2 97.7 %all-gather.22.cloned.1.call-start = ((), (), s32[]{:S(2)}) async-start(), calls=%async_computation.5 | async-start | bytes 2359296 | tf_op jit(solution)/shard_map/all_gather | solution.py:267
  693.3 145.5 %all-gather.26.cloned.1.call-start = ((), (), s32[]{:S(2)}) async-start(), calls=%async_computation.7 | async-start | bytes 2359296 | tf_op jit(solution)/shard_map/all_gather | solution.py:379
  693.9 195.2 %all-gather.24.cloned.1.call-start = ((), (), s32[]{:S(2)}) async-start(), calls=%async_computation.6 | async-start | bytes 2359296 | tf_op jit(solution)/shard_map/all_gather | solution.py:379
  694.7 265.9 %all-gather.28.cloned.1.call-start = ((), (), s32[]{:S(2)}) async-start(), calls=%async_computation.11 | async-start | bytes 2359296 | tf_op jit(solution)/shard_map/all_gather | solution.py:380
  800.5 280.9 %copy-start.4 = (f32[1,128,1024]{2,1,0:T(8,128)}, f32[1,128,1024]{2,1,0:T(8,128)S(1)}, u32[]{:S(2)}) copy-start(f32[1,128,1024]{2,1,0:T(8,128)S(1)} %get-tuple-element.84) | copy-start | bytes 1572868
  821.0 324.1 %all-gather.30.cloned.1.call-start = ((), (), s32[]{:S(2)}) async-start(), calls=%async_computation.12 | async-start | bytes 2359296 | tf_op jit(solution)/shard_map/all_gather | solution.py:380
  822.2 149.2 %copy-start.102 = (f32[128]{0:T(128)}, f32[128]{0:T(128)S(1)}, u32[]{:S(2)}) copy-start(f32[128]{0:T(128)S(1)} %multiply_bitcast_fusion) | copy-start | bytes 1540
  1013.9 1115.4 %reduce-scatter.2.cloned.1.call-start = ((), (), s32[]{:S(2)}) async-start(), calls=%async_computation.8 | async-start | bytes 56623104 | tf_op jit(solution)/shard_map/reduce_scatter | solution.py:443
  1100.7 36.2 %copy-start.15 = (bf16[1,1024,1024]{1,2,0:T(8,128)(2,1)S(1)}, bf16[1,1024,1024]{1,2,0:T(8,128)(2,1)}, u32[]{:S(2)}) copy-start(bf16[1,1024,1024]{1,2,0:T(8,128)(2,1)} %copy.103) | copy-start | bytes 6291460
  1321.3 934.6 %all-reduce.5.cloned.1.call-start = ((), (), s32[]{:S(2)}) async-start(), calls=%async_computation.10 | async-start | bytes 196608 | tf_op jit(solution)/shard_map/psum | solution.py:445
  1330.0 997.6 %all-reduce.3.cloned.1.call-start = ((), (), s32[]{:S(2)}) async-start(), calls=%async_computation.9 | async-start | bytes 6291456 | tf_op jit(solution)/shard_map/psum | solution.py:444
  1330.1 804.2 %copy-start.5 = (f32[1,128,1024]{2,1,0:T(8,128)S(1)}, f32[1,128,1024]{2,1,0:T(8,128)}, u32[]{:S(2)}) copy-start(f32[1,128,1024]{2,1,0:T(8,128)} %copy-done.4) | copy-start | bytes 1572868
  1330.1 804.2 %copy-start.92 = (f32[1,1024]{1,0:T(1,128)S(1)}, f32[1,1024]{1,0:T(1,128)}, u32[]{:S(2)}) copy-start(f32[1,1024]{1,0:T(1,128)} %copy-done.91) | copy-start | bytes 12292
  2134.3 122.7 %copy-start.62 = (f32[20,1024]{1,0:T(8,128)S(1)}, f32[20,1024]{1,0:T(8,128)}, u32[]{:S(2)}) copy-start(f32[20,1024]{1,0:T(8,128)} %param.20) | copy-start | bytes 245764
  2134.3 122.7 %copy-start.63 = (f32[20,1024]{1,0:T(8,128)S(1)}, f32[20,1024]{1,0:T(8,128)}, u32[]{:S(2)}) copy-start(f32[20,1024]{1,0:T(8,128)} %param.21) | copy-start | bytes 245764
  2258.6 71.7 %copy-start.67 = (f32[24,256]{1,0:T(8,128)S(1)}, f32[24,256]{1,0:T(8,128)}, u32[]{:S(2)}) copy-start(f32[24,256]{1,0:T(8,128)} %param.19) | copy-start | bytes 73732
  2330.3 242.2 %copy-start.1 = (f32[24,256,256]{2,1,0:T(8,128)}, f32[24,256,256]{2,1,0:T(8,128)S(1)}, u32[]{:S(2)}) copy-start(f32[24,256,256]{2,1,0:T(8,128)S(1)} %get-tuple-element.115) | copy-start | bytes 18874372
  2341.5 47.7 %copy-start.17 = (f32[24,256,256]{2,1,0:T(8,128)}, f32[24,256,256]{2,1,0:T(8,128)S(1)}, u32[]{:S(2)}) copy-start(f32[24,256,256]{2,1,0:T(8,128)S(1)} %get-tuple-element.117) | copy-start | bytes 18874372
  (107 other events, 893.5 us)
Sparse Core Ops, SparseCore 0:
  15.2 481.6 all-gather.13
  566.1 48.1 all-gather.15
  617.1 47.7 all-gather.17
  691.4 47.7 all-gather.19
  741.1 47.7 all-gather.21
  790.9 47.8 all-gather.25
  841.0 48.0 all-gather.23
  891.2 48.4 all-gather.27
  1014.0 60.4 all-gather.29
  1321.5 807.8 reduce-scatter.1
  2136.5 119.4 all-reduce.4
  2258.8 68.7 all-reduce.2
where the time goes:
time: 2780 us; the launch traced here: 2770 us
  waiting for transfers between devices  1560 us (56%)
  matrix products  619 us (22%)
  local copies, waits for them, and re-layouts  316 us (11%)
  other arithmetic  134 us (5%)
  blocking collectives  117 us (4%)
    reduce_scatter x1, waiting for transfers between devices, local(): shared = lax.psum_scatter(slotted, 'blk', scatter_dimension=0, tiled=True)  799 us
    all_gather x1, waiting for transfers between devices, local(): lax.all_gather(masters.astype(jnp.bfloat16), 'blk', axis=0, tiled=True)  479 us
    dot_general x12, matrix products, invert_root(): approx = jnp.dot(approx, factor, precision=HIGH)  128 us
    psum x1, waiting for transfers between devices, local(): vec_grads = lax.psum(vec_one + vec_two, ('samp', 'blk'))  111 us
    dot_general x10, matrix products, invert_root(): jnp.dot(jnp.dot(square, square, precision=HIGH), moving, precision=HIGH)  93.5 us
    dot_general x10, matrix products, invert_root(): square = jnp.dot(factor, factor, precision=HIGH)  81.3 us
    dot_general x10, matrix products, invert_root(): jnp.dot(square, square, precision=HIGH)  80.8 us
    reshape x6, local copies, waits for them, and re-layouts, carve(): matrix.reshape(height // BS, BS, breadth // BS, BS).transpose(0, 2, 1, 3)  72.9 us
  transfers between devices with their start and end apart: 12, of which 9 were waited for; matrix products, arithmetic and copies ran while one was open for 11% of the time, Pallas kernels for 0%

commit v1 on v0

--- a/solution.py
+++ b/solution.py
@@ -1,8 +1,12 @@
+import functools
 import math
 
 import jax
+import ml_dtypes
 import jax.numpy as jnp
 from jax import lax
+from jax.experimental import pallas as pl
+from jax.experimental.pallas import tpu as pltpu
 from jax.sharding import PartitionSpec as P
 
 D = 1024
@@ -218,7 +222,434 @@
     return (left_new, right_new, weight - step_rate * ratio * direction)
 
 
-def local(
+MESH = pl.DeviceIdType.MESH
+LOW = jnp.bfloat16
+FULL = jnp.float32
+VMEM_ASK = 60 * 1024 * 1024
+GROUP = 24
+HALF = 12
+QUART = 4
+
+
+def place():
+    samp = lax.axis_index("samp")
+    blk = lax.axis_index("blk")
+    return (lax.div(samp, 2), lax.rem(samp, 2), lax.div(blk, 2), lax.rem(blk, 2))
+
+
+def meet(devices):
+    barrier = pltpu.get_barrier_semaphore()
+    for device in devices:
+        pl.semaphore_signal(barrier, inc=1, device_id=device, device_id_type=MESH)
+    pl.semaphore_wait(barrier, len(devices))
+
+
+def meet_all():
+    barrier = pltpu.get_barrier_semaphore()
+    samp = lax.axis_index("samp")
+    blk = lax.axis_index("blk")
+
+    def tell(at, carry):
+        to = lax.rem(samp * 8 + blk + at, 32)
+        pl.semaphore_signal(
+            barrier, inc=1, device_id=(lax.div(to, 8), lax.rem(to, 8)), device_id_type=MESH
+        )
+        return carry
+
+    lax.fori_loop(1, 32, tell, 0)
+    pl.semaphore_wait(barrier, 31)
+
+
+def turned_pair(n):
+    return 2 * lax.rem(n, 2) + lax.div(n, 2)
+
+
+class Swap:
+    def __init__(self, local_sems, send_sems, recv_sems):
+        x, c, z, y = place()
+        self.stays = z == turned_pair(2 * x + c)
+        self.to = (turned_pair(z), 2 * turned_pair(2 * x + c) + y)
+        self.sems = (local_sems, send_sems, recv_sems)
+        self.pairs = []
+
+    def start(self, src, dst):
+        at = len(self.pairs)
+        local_sems, send_sems, recv_sems = self.sems
+        local = pltpu.make_async_copy(src, dst, local_sems.at[at])
+        away = pltpu.make_async_remote_copy(
+            src_ref=src, dst_ref=dst, send_sem=send_sems.at[at], recv_sem=recv_sems.at[at],
+            device_id=self.to, device_id_type=MESH,
+        )
+        self.pairs.append((local, away))
+
+        @pl.when(self.stays)
+        def keep():
+            local.start()
+
+        @pl.when(jnp.logical_not(self.stays))
+        def send():
+            away.start()
+
+    def finish(self):
+        @pl.when(self.stays)
+        def kept():
+            for local, away in self.pairs:
+                local.wait()
+
+        @pl.when(jnp.logical_not(self.stays))
+        def sent():
+            for local, away in self.pairs:
+                away.wait()
+
+
+def push(src, dst, send, recv, device):
+    copy = pltpu.make_async_remote_copy(
+        src_ref=src, dst_ref=dst, send_sem=send, recv_sem=recv, device_id=device, device_id_type=MESH
+    )
+    copy.start()
+    return copy
+
+
+FIRST, SECOND, BOTH, CROSS = range(4)
+SIZES = (2, 2, 3, 1)
+
+
+def weights_kernel(
+    masters, notes, rows_in, out, notes_out, rows_out,
+    wide, low, load_sems, local_sems, z_sems, y_sems, x_sems, core_sems, far_sems,
+    swap_local, swap_send, swap_recv, note_send, note_recv,
+):
+    x, c, z, y = place()
+    samp = 2 * x + c
+    blk = 2 * z + y
+    to_y = (samp, 2 * z + 1 - y)
+    to_x = (2 * (1 - x) + c, blk)
+    to_c = (2 * x + 1 - c, blk)
+    base = c * HALF
+    starts = (base + x * 8, base + x * 8 + 2, base + QUART, base + QUART + 3)
+    far_starts = (base + (1 - x) * 8, base + (1 - x) * 8 + 2)
+    parts = [
+        (base + x * 8, QUART), (base + QUART, QUART), (base + (1 - x) * 8, QUART), ((1 - c) * HALF, HALF),
+    ]
+    loads = []
+    for at, (start, size) in enumerate(parts):
+        loads.append(
+            pltpu.make_async_copy(masters.at[pl.ds(start, size)], wide.at[pl.ds(start, size)], load_sems.at[at])
+        )
+        loads[-1].start()
+    meet_all()
+    swap = Swap(swap_local, swap_send, swap_recv)
+    swap.start(rows_in, rows_out)
+    keeps = []
+
+    def ready(at):
+        start, size = parts[at]
+        loads[at].wait()
+        low[pl.ds(start, size)] = wide[pl.ds(start, size)].astype(LOW)
+        keeps.append(
+            pltpu.make_async_copy(
+                low.at[pl.ds(start, size)], out.at[pl.ds(blk * GROUP + start, size)], local_sems.at[at]
+            )
+        )
+        keeps[-1].start()
+
+    def copy(src, group, start, size, sems, at, device):
+        place_out = out.at[pl.ds(group * GROUP + start, size)]
+        return pltpu.make_async_remote_copy(
+            src_ref=place_out if src is None else src, dst_ref=place_out,
+            send_sem=sems.at[(0,) + at], recv_sem=sems.at[(1,) + at], device_id=device, device_id_type=MESH,
+        )
+
+    def mine(kind):
+        return low.at[pl.ds(starts[kind], SIZES[kind])]
+
+    def z_copy(kind, way, origin, own=False):
+        group = 2 * origin + y
+        to = (samp, blk + (2 if way == 0 else -2))
+        return copy(mine(kind) if own else None, group, starts[kind], SIZES[kind], z_sems, (kind, way, origin), to)
+
+    def z_cross(way, origin, side, own=False):
+        group = 2 * origin + side
+        to = (samp, blk + (2 if way == 0 else -2))
+        return copy(
+            mine(CROSS) if own else None, group, starts[CROSS], 1, z_sems, (CROSS + side, way, origin), to
+        )
+
+    def y_copy(kind, origin, own=False):
+        group = 2 * origin + y
+        return copy(mine(kind) if own else None, group, starts[kind], SIZES[kind], y_sems, (kind, origin), to_y)
+
+    def y_landed(kind, origin):
+        group = 2 * origin + 1 - y
+        return copy(None, group, starts[kind], SIZES[kind], y_sems, (kind, origin), to_y)
+
+    def x_copy(kind, group):
+        return copy(None, group, starts[kind], SIZES[kind], x_sems, (kind, group), to_x)
+
+    def x_landed(kind, group):
+        return copy(None, group, far_starts[kind], SIZES[kind], x_sems, (kind, group), to_x)
+
+    def core_copy(kind, group):
+        return copy(None, group, starts[kind], SIZES[kind], core_sems, (kind, group), to_c)
+
+    def far_copy(kind, group):
+        return copy(None, group, far_starts[kind], SIZES[kind], far_sems, (kind, group), to_c)
+
+    def on_from_here(kind, group):
+        if kind in (FIRST, SECOND):
+            x_copy(kind, group).start()
+        core_copy(kind, group).start()
+
+    def begin(kind):
+        @pl.when(z < 3)
+        def up():
+            z_copy(kind, 0, z, True).start()
+
+        @pl.when(z > 0)
+        def down():
+            z_copy(kind, 1, z, True).start()
+
+        y_copy(kind, z, True).start()
+
+    def z_step(kind, distance):
+        for way in (0, 1):
+            origin = z - distance if way == 0 else z + distance
+
+            @pl.when(origin >= 0 if way == 0 else origin <= 3)
+            def arrived():
+                z_copy(kind, way, origin).wait_recv()
+
+                @pl.when(z < 3 if way == 0 else z > 0)
+                def onward():
+                    z_copy(kind, way, origin).start()
+
+                y_copy(kind, origin).start()
+                on_from_here(kind, 2 * origin + y)
+
+    def y_step(kind, distance):
+        for way in (0, 1):
+            origin = z - distance if way == 0 else z + distance
+
+            @pl.when(origin >= 0 if way == 0 else origin <= 3)
+            def arrived():
+                y_landed(kind, origin).wait_recv()
+                on_from_here(kind, 2 * origin + 1 - y)
+
+    def y_own(kind):
+        y_landed(kind, z).wait_recv()
+        on_from_here(kind, 2 * z + 1 - y)
+
+    def cross_step(distance):
+        for side in (0, 1):
+            for way in (0, 1):
+                origin = z - distance if way == 0 else z + distance
+
+                @pl.when(origin >= 0 if way == 0 else origin <= 3)
+                def arrived():
+                    z_cross(way, origin, side).wait_recv()
+
+                    @pl.when(z < 3 if way == 0 else z > 0)
+                    def onward():
+                        z_cross(way, origin, side).start()
+
+                    core_copy(CROSS, 2 * origin + side).start()
+
+    def x_step(kind, distance, same):
+        for way in (0, 1):
+            origin = z - distance if way == 0 else z + distance
+
+            @pl.when(origin >= 0 if way == 0 else origin <= 3)
+            def arrived():
+                group = 2 * origin + (y if same else 1 - y)
+                x_landed(kind, group).wait_recv()
+                far_copy(kind, group).start()
+
+    def x_own(kind):
+        x_landed(kind, 2 * z + 1 - y).wait_recv()
+        far_copy(kind, 2 * z + 1 - y).start()
+
+    note_local = pltpu.make_async_copy(notes, notes_out.at[blk], local_sems.at[4])
+
+    def note_copy(j, origin):
+        return pltpu.make_async_remote_copy(
+            src_ref=notes, dst_ref=notes_out.at[origin], send_sem=note_send.at[j], recv_sem=note_recv.at[origin],
+            device_id=(j // 2, 2 * turned_pair(samp) + j % 2), device_id_type=MESH,
+        )
+
+    stays = z == turned_pair(samp)
+
+    def is_me(j):
+        return jnp.logical_and(stays, 2 * samp + y == j)
+
+    def here_from(j):
+        return jnp.logical_and(stays, blk == j)
+
+    ready(0)
+    begin(FIRST)
+    begin(SECOND)
+    ready(1)
+    y_copy(CROSS, z, True).start()
+    for j in range(8):
+
+        @pl.when(jnp.logical_not(is_me(j)))
+        def send_note():
+            note_copy(j, blk).start()
+
+    @pl.when(stays)
+    def keep_note():
+        note_local.start()
+
+    ready(2)
+    ready(3)
+    z_step(FIRST, 1)
+    y_own(FIRST)
+    z_step(SECOND, 1)
+    y_own(SECOND)
+    begin(BOTH)
+    y_landed(CROSS, z).wait_recv()
+    core_copy(CROSS, 2 * z + 1 - y).start()
+    for way, there in ((0, z < 3), (1, z > 0)):
+        for side in (0, 1):
+            @pl.when(jnp.logical_and(there, y == side))
+            def own_side():
+                z_cross(way, z, side, True).start()
+
+            @pl.when(jnp.logical_and(there, y != side))
+            def other_side():
+                z_cross(way, z, side).start()
+
+    z_step(FIRST, 2)
+    y_step(FIRST, 1)
+    z_step(SECOND, 2)
+    y_step(SECOND, 1)
+    x_own(FIRST)
+    z_step(FIRST, 3)
+    x_own(SECOND)
+    y_step(FIRST, 2)
+    z_step(SECOND, 3)
+    x_step(FIRST, 1, True)
+    y_step(SECOND, 2)
+    x_step(SECOND, 1, True)
+    y_step(FIRST, 3)
+    y_step(SECOND, 3)
+    z_step(BOTH, 1)
+    x_step(FIRST, 1, False)
+    x_step(FIRST, 2, True)
+    y_own(BOTH)
+    cross_step(1)
+    x_step(SECOND, 1, False)
+    x_step(SECOND, 2, True)
+    z_step(BOTH, 2)
+    x_step(FIRST, 3, True)
+    y_step(BOTH, 1)
+    cross_step(2)
+    x_step(FIRST, 2, False)
+    z_step(BOTH, 3)
+    x_step(SECOND, 3, True)
+    y_step(BOTH, 2)
+    x_step(SECOND, 2, False)
+    cross_step(3)
+    x_step(FIRST, 3, False)
+    y_step(BOTH, 3)
+    x_step(SECOND, 3, False)
+
+    other = (1 - c) * HALF
+    other_starts = (other + x * 8, other + x * 8 + 2, other + QUART, other + QUART + 3)
+    other_far = (other + (1 - x) * 8, other + (1 - x) * 8 + 2)
+
+    def settle(group, carry):
+        @pl.when(group != blk)
+        def other_group():
+            for kind in range(4):
+                copy(None, group, other_starts[kind], SIZES[kind], core_sems, (kind, group), to_c).wait_recv()
+                core_copy(kind, group).wait_send()
+            for kind in (FIRST, SECOND):
+                copy(None, group, other_far[kind], SIZES[kind], far_sems, (kind, group), to_c).wait_recv()
+                far_copy(kind, group).wait_send()
+                x_copy(kind, group).wait_send()
+
+        return carry
+
+    lax.fori_loop(0, 8, settle, 0)
+
+    def sent_along(origin, carry):
+        for kind in (FIRST, SECOND, BOTH):
+            y_copy(kind, origin).wait_send()
+
+            @pl.when(jnp.logical_and(origin <= z, z < 3))
+            def up():
+                z_copy(kind, 0, origin).wait_send()
+
+            @pl.when(jnp.logical_and(origin >= z, z > 0))
+            def down():
+                z_copy(kind, 1, origin).wait_send()
+
+        for side in (0, 1):
+            @pl.when(jnp.logical_and(origin <= z, z < 3))
+            def cross_up():
+                z_cross(0, origin, side).wait_send()
+
+            @pl.when(jnp.logical_and(origin >= z, z > 0))
+            def cross_down():
+                z_cross(1, origin, side).wait_send()
+
+        return carry
+
+    lax.fori_loop(0, 4, sent_along, 0)
+    y_copy(CROSS, z).wait_send()
+    for keep in keeps:
+        keep.wait()
+    swap.finish()
+    for j in range(8):
+
+        @pl.when(jnp.logical_not(is_me(j)))
+        def sent_note():
+            note_copy(j, blk).wait_send()
+
+        @pl.when(jnp.logical_not(here_from(j)))
+        def got_note():
+            note_copy(j, j).wait_recv()
+
+    @pl.when(stays)
+    def kept_note():
+        note_local.wait()
+
+
+def gather_weights(masters, notes, rows):
+    any_at = pl.BlockSpec(memory_space=pl.ANY)
+    return pl.pallas_call(
+        weights_kernel,
+        out_shape=(
+            jax.ShapeDtypeStruct((NB, BS, BS), LOW),
+            jax.ShapeDtypeStruct((8,) + notes.shape, notes.dtype),
+            jax.ShapeDtypeStruct(rows.shape, rows.dtype),
+        ),
+        in_specs=[any_at] * 3,
+        out_specs=[any_at] * 3,
+        scratch_shapes=[
+            pltpu.VMEM((GROUP, BS, BS), FULL),
+            pltpu.VMEM((GROUP, BS, BS), LOW),
+            pltpu.SemaphoreType.DMA((4,)),
+            pltpu.SemaphoreType.DMA((5,)),
+            pltpu.SemaphoreType.DMA((2, 5, 2, 4)),
+            pltpu.SemaphoreType.DMA((2, 4, 4)),
+            pltpu.SemaphoreType.DMA((2, 2, 8)),
+            pltpu.SemaphoreType.DMA((2, 4, 8)),
+            pltpu.SemaphoreType.DMA((2, 2, 8)),
+            pltpu.SemaphoreType.DMA((1,)),
+            pltpu.SemaphoreType.DMA((1,)),
+            pltpu.SemaphoreType.DMA((1,)),
+            pltpu.SemaphoreType.DMA((8,)),
+            pltpu.SemaphoreType.DMA((8,)),
+        ],
+        compiler_params=pltpu.CompilerParams(
+            collective_id=0, has_side_effects=True, vmem_limit_bytes=VMEM_ASK
+        ),
+        name="gather_weights",
+    )(masters, notes, rows)
+
+
+def local_any(
     inputs,
     cot_first,
     cot_second,
@@ -466,6 +897,1172 @@
     )
 
 
+TOKENS = 128
+PAIR = 2 * HD
+SEQ_ALL = 8 * TOKENS
+QKV_AT, OUT_AT, UP_AT, DOWN_AT = 0, 48, 64, 128
+WIDE = D // BS
+DEEP = FF // BS
+LEAD_AT = 8 + FF // D
+
+
+def dot(left, right):
+    return jnp.dot(left, right, preferred_element_type=FULL)
+
+
+def dot_t(left, right):
+    return lax.dot_general(left, right, (((1,), (1,)), ((), ())), preferred_element_type=FULL)
+
+
+def fetch(copies, slots, base, rows, cols, target, sem):
+    def start(at, carry):
+        row = lax.div(at, cols)
+        pltpu.make_async_copy(
+            copies.at[slots[base + at]], target(row, at - row * cols), sem
+        ).start()
+        return carry
+
+    lax.fori_loop(0, rows * cols, start, 0)
+
+
+def fetch_qkv(copies, slots, held, sem):
+    fetch(copies, slots, QKV_AT, WIDE, 3 * WIDE, lambda k, n: held.at[n, pl.ds(k * BS, BS)], sem)
+
+
+def fetch_out(copies, slots, held, sem):
+    fetch(
+        copies, slots, OUT_AT, WIDE, WIDE, lambda k, n: held.at[pl.ds(k * BS, BS), pl.ds(n * BS, BS)], sem
+    )
+
+
+def fetch_up(copies, slots, held, sem):
+    fetch(copies, slots, UP_AT, WIDE, DEEP, lambda k, n: held.at[n, pl.ds(k * BS, BS)], sem)
+
+
+def fetch_down(copies, slots, held, sem):
+    fetch(copies, slots, DOWN_AT, DEEP, WIDE, lambda k, n: held.at[k, :, pl.ds(n * BS, BS)], sem)
+
+
+def landed(held, sem):
+    pltpu.make_async_copy(held, held, sem).wait()
+
+
+def normal(value):
+    centred = value - jnp.mean(value, axis=-1, keepdims=True)
+    rate = lax.rsqrt(jnp.mean(centred * centred, axis=-1, keepdims=True) + 1e-06)
+    return (centred * rate, rate)
+
+
+def normal_back(grad, unit, rate, gain):
+    scaled = grad * gain
+    return rate * (
+        scaled
+        - jnp.mean(scaled, axis=-1, keepdims=True)
+        - unit * jnp.mean(scaled * unit, axis=-1, keepdims=True)
+    )
+
+
+def total(value):
+    return jnp.sum(value, axis=0, keepdims=True)
+
+
+def gelu_parts(value):
+    phi = 0.5 + 0.5 * lax.erf(value * (0.5**0.5))
+    return phi, value * phi
+
+
+def gelu_slope(value):
+    phi, unused = gelu_parts(value)
+    return phi + value * jnp.exp(-0.5 * value * value) * ((2.0 * math.pi) ** -0.5)
+
+
+def project(hidden, vecs, qkv, a_out, packed_out):
+    unit, unused = normal(hidden)
+    normed = unit * vecs[0:1] + vecs[1:2]
+    for k in range(WIDE):
+        a_out[k] = normed[:, k * BS : (k + 1) * BS].T.astype(LOW)
+    normed = normed.astype(LOW)
+    for n in range(3 * WIDE):
+        part = dot(normed, qkv[n])
+        kind, within = divmod(n, WIDE)
+        if kind != 1:
+            row = 2 if kind == 0 else 3
+            part = part + vecs[row : row + 1, within * BS : (within + 1) * BS]
+        part = part.astype(LOW)
+        for half in range(2):
+            packed_out[2 * within + half, :, kind * PAIR : (kind + 1) * PAIR] = part[
+                :, half * PAIR : (half + 1) * PAIR
+            ]
+
+
+def feed(hidden, o_in, vecs, out_w, up, down, sems, o_out, n2_out, act_out, u_out, act_held):
+    landed(out_w, sems.at[0])
+    attended = jnp.concatenate([o_in[j] for j in range(8)], axis=1)
+    for k in range(WIDE):
+        o_out[k] = attended[:, k * BS : (k + 1) * BS].astype(FULL).T.astype(LOW)
+    middle = hidden + dot(attended, out_w[...]) + vecs[4:5]
+    unit, unused = normal(middle)
+    normed = unit * vecs[5:6] + vecs[6:7]
+    for k in range(WIDE):
+        n2_out[k] = normed[:, k * BS : (k + 1) * BS].T.astype(LOW)
+    normed = normed.astype(LOW)
+    landed(up, sems.at[1])
+    per = D // BS
+    for f in range(DEEP):
+        bias = vecs[8 + f // per : 9 + f // per, (f % per) * BS : (f % per + 1) * BS]
+        upward = dot(normed, up[f]) + bias
+        u_out[f] = upward
+        activated = gelu_parts(upward)[1]
+        act_held[f] = activated.astype(LOW)
+        act_out[f] = activated.T.astype(LOW)
+    landed(down, sems.at[2])
+    result = middle + vecs[7:8]
+    for f in range(DEEP):
+        result = result + dot(act_held[f], down[f])
+    return middle, result
+
+
+def feed_back(grad_out, middle, u_in, vecs, out_w, up, down, du_out, dz1_out, dz2_out, do_out, rows):
+    grad_two = grad_out.astype(LOW)
+    for k in range(WIDE):
+        dz2_out[k] = grad_two[:, k * BS : (k + 1) * BS]
+    rows[7:8] += total(grad_two.astype(FULL))
+    per = D // BS
+    grad_normed = None
+    for f in range(DEEP):
+        grad_act = dot_t(grad_two, down[f])
+        grad_up = (grad_act * gelu_slope(u_in[f])).astype(LOW)
+        du_out[f] = grad_up
+        rows[8 + f // per : 9 + f // per, (f % per) * BS : (f % per + 1) * BS] += total(
+            grad_up.astype(FULL)
+        )
+        term = dot_t(grad_up, up[f])
+        grad_normed = term if grad_normed is None else grad_normed + term
+    unit, rate = normal(middle)
+    rows[5:6] += total(grad_normed * unit)
+    rows[6:7] += total(grad_normed)
+    grad_middle = grad_out + normal_back(grad_normed, unit, rate, vecs[5:6])
+    grad_one = grad_middle.astype(LOW)
+    for k in range(WIDE):
+        dz1_out[k] = grad_one[:, k * BS : (k + 1) * BS]
+    rows[4:5] += total(grad_one.astype(FULL))
+    grad_attended = dot_t(grad_one, out_w[...]).astype(LOW)
+    for j in range(8):
+        do_out[j] = grad_attended[:, j * PAIR : (j + 1) * PAIR]
+    return grad_middle
+
+
+def project_back(grad_middle, hidden, dq_in, dkv_in, vecs, qkv, dqkv_out, rows, lead):
+    grad_normed = None
+    for n in range(3 * WIDE):
+        kind, within = divmod(n, WIDE)
+        source, cols = (dq_in, slice(0, PAIR)) if kind == 0 else (dkv_in, slice((kind - 1) * PAIR, kind * PAIR))
+        part = jnp.concatenate([source[2 * within, :, cols], source[2 * within + 1, :, cols]], axis=1)
+        dqkv_out[n] = part
+        if kind != 1:
+            row = 2 if kind == 0 else 3
+            rows[row : row + 1, within * BS : (within + 1) * BS] += total(part.astype(FULL))
+        term = dot_t(part, qkv[n])
+        grad_normed = term if grad_normed is None else grad_normed + term
+    unit, rate = normal(hidden)
+    rows[0:1] += total(grad_normed * unit)
+    rows[1:2] += total(grad_normed)
+    grad_hidden = grad_middle + normal_back(grad_normed, unit, rate, vecs[0:1])
+    rows[pl.ds(LEAD_AT + lead, 1)] += total(grad_hidden)
+    return grad_hidden
+
+
+def first_kernel(slots, leads, x, vecs, copies, h_out, a_out, packed_out, qkv, sems):
+    fetch_qkv(copies, slots, qkv, sems.at[0])
+    hidden = x[0].astype(FULL) + vecs[pl.ds(LEAD_AT + leads[0, 0], 1)]
+    h_out[...] = hidden
+    landed(qkv, sems.at[0])
+    project(hidden, vecs, qkv, a_out, packed_out)
+
+
+def between_kernel(
+    slots, leads, h_in, o_in, vecs, copies,
+    m_out, u_out, o_out, n2_out, act_out, y_out, h_out, a_out, packed_out,
+    out_w, up, down, qkv, act_held, sems,
+):
+    fetch_out(copies, slots, out_w, sems.at[0])
+    fetch_up(copies, slots, up, sems.at[1])
+    fetch_down(copies, slots, down, sems.at[2])
+    fetch_qkv(copies, slots, qkv, sems.at[3])
+    middle, result = feed(
+        h_in[...], o_in, vecs, out_w, up, down, sems, o_out, n2_out, act_out, u_out, act_held
+    )
+    m_out[...] = middle
+    y_out[0] = result.astype(LOW)
+    hidden = result + vecs[pl.ds(LEAD_AT + leads[1, 0], 1)]
+    h_out[...] = hidden
+    landed(qkv, sems.at[3])
+    project(hidden, vecs, qkv, a_out, packed_out)
+
+
+def turn_kernel(
+    slots, h_in, o_in, cot, vecs, copies,
+    o_out, n2_out, act_out, y_out, du_out, dz1_out, dz2_out, do_out, dm_out, rows,
+    out_w, up, down, u_held, act_held, sems,
+):
+    fetch_out(copies, slots, out_w, sems.at[0])
+    fetch_up(copies, slots, up, sems.at[1])
+    fetch_down(copies, slots, down, sems.at[2])
+    middle, result = feed(
+        h_in[...], o_in, vecs, out_w, up, down, sems, o_out, n2_out, act_out, u_held, act_held
+    )
+    y_out[0] = result.astype(LOW)
+    rows[...] = jnp.zeros_like(rows)
+    dm_out[...] = feed_back(
+        cot[0].astype(FULL), middle, u_held, vecs, out_w, up, down, du_out, dz1_out, dz2_out, do_out, rows
+    )
+
+
+def back_between_kernel(
+    slots, leads, dm_in, h_in, dq_in, dkv_in, rows_in, cot, m_in, u_in, vecs, copies,
+    dqkv_out, du_out, dz1_out, dz2_out, do_out, dm_out, rows,
+    out_w, up, down, qkv, sems,
+):
+    fetch_qkv(copies, slots, qkv, sems.at[3])
+    fetch_down(copies, slots, down, sems.at[2])
+    fetch_up(copies, slots, up, sems.at[1])
+    fetch_out(copies, slots, out_w, sems.at[0])
+    rows[...] = rows_in[...]
+    landed(qkv, sems.at[3])
+    grad = project_back(dm_in[...], h_in[...], dq_in, dkv_in, vecs, qkv, dqkv_out, rows, leads[1, 0])
+    grad = grad + cot[0].astype(FULL)
+    landed(down, sems.at[2])
+    landed(up, sems.at[1])
+    landed(out_w, sems.at[0])
+    dm_out[...] = feed_back(
+        grad, m_in[...], u_in, vecs, out_w, up, down, du_out, dz1_out, dz2_out, do_out, rows
+    )
+
+
+def last_kernel(
+    slots, leads, dm_in, h_in, dq_in, dkv_in, rows_in, vecs, copies, dqkv_out, grad_out, rows, qkv, sems
+):
+    fetch_qkv(copies, slots, qkv, sems.at[0])
+    rows[...] = rows_in[...]
+    landed(qkv, sems.at[0])
+    grad_out[0] = project_back(
+        dm_in[...], h_in[...], dq_in, dkv_in, vecs, qkv, dqkv_out, rows, leads[0, 0]
+    ).astype(LOW)
+
+
+SMEM_IN = pl.BlockSpec(memory_space=pltpu.SMEM)
+VMEM_AT = pl.BlockSpec(memory_space=pltpu.VMEM)
+ANY_AT = pl.BlockSpec(memory_space=pl.ANY)
+
+
+def shape(dims, kind=LOW):
+    return jax.ShapeDtypeStruct(dims, kind)
+
+
+HELD = {
+    "qkv": pltpu.VMEM((3 * WIDE, D, BS), LOW),
+    "out": pltpu.VMEM((D, D), LOW),
+    "up": pltpu.VMEM((DEEP, D, BS), LOW),
+    "down": pltpu.VMEM((DEEP, BS, D), LOW),
+}
+SHAPES = {
+    "wide": shape((TOKENS, D), FULL),
+    "four": shape((WIDE, TOKENS, BS)),
+    "four_t": shape((WIDE, BS, TOKENS)),
+    "sixteen_t": shape((DEEP, BS, TOKENS)),
+    "double": shape((8, TOKENS, 2 * PAIR)),
+    "stats": shape((8, SEQ_ALL), FULL),
+    "turned": shape((SEQ_ALL // BS, PAIR, BS), FULL),
+    "twelve": shape((3 * WIDE, TOKENS, BS)),
+    "sixteen": shape((DEEP, TOKENS, BS)),
+    "up": shape((DEEP, TOKENS, BS), FULL),
+    "packed": shape((8, TOKENS, 3 * PAIR)),
+    "pair": shape((8, TOKENS, PAIR)),
+    "pred": shape((1, TOKENS, D)),
+    "rows": shape((20, D), FULL),
+}
+
+
+def plain(kernel, specs, outs, held, flops, name, extra=()):
+    return pl.pallas_call(
+        kernel,
+        out_shape=tuple(SHAPES[out] for out in outs),
+        in_specs=specs,
+        out_specs=tuple(VMEM_AT for out in outs),
+        scratch_shapes=[HELD[part] for part in held] + list(extra) + [pltpu.SemaphoreType.DMA((4,))],
+        compiler_params=pltpu.CompilerParams(vmem_limit_bytes=VMEM_ASK),
+        cost_estimate=pl.CostEstimate(flops=flops, bytes_accessed=24 << 20, transcendentals=0),
+        name=name,
+    )
+
+
+def bias_pieces():
+    left = masked
+    pieces = []
+    for unused in range(3):
+        piece = float(ml_dtypes.bfloat16(left))
+        pieces.append(piece)
+        left -= piece
+    assert left == 0.0
+    return pieces
+
+
+MASK_PIECES = bias_pieces()
+
+
+def head_sides(queries, keys, neg, head):
+    lane = lax.broadcasted_iota(jnp.int32, queries.shape, 1)
+    own = (lane < HD) if head == 0 else (lane >= HD)
+    spot = lane - (HD if head == 0 else 0)
+    key_side = jnp.zeros_like(keys)
+    for at, piece in enumerate(MASK_PIECES):
+        key_side = jnp.where(spot == at, neg * piece, key_side)
+    key_side = jnp.where(own, keys, key_side)
+    ones = jnp.where((spot >= 0) & (spot < 3), 1.0, 0.0)
+    query_side = jnp.where(own, queries * HD**-0.5, ones)
+    return query_side, key_side, own
+
+
+class Plane:
+    def __init__(self):
+        x, c, z, y = place()
+        self.z = z
+        self.me = 4 * c + 2 * x + y
+
+    def device(self, j):
+        return (turned_pair(lax.div(j, 2)), 2 * self.z + lax.rem(j, 2))
+
+    def other(self, step):
+        return lax.rem(self.me + step, 8)
+
+    def others(self):
+        return [self.device(self.other(step)) for step in range(1, 8)]
+
+    def copy(self, src, dst, sems, send_at, recv_at, to):
+        return pltpu.make_async_remote_copy(
+            src_ref=src, dst_ref=dst, send_sem=sems.at[0, send_at], recv_sem=sems.at[1, recv_at],
+            device_id=self.device(to), device_id_type=MESH,
+        )
+
+    def send(self, source, target, sems, to):
+        self.copy(source.at[to], target.at[self.me], sems, to, self.me, to).start()
+
+    def send_or_keep(self, source, target, sems, to):
+        @pl.when(to != self.me)
+        def away():
+            self.send(source, target, sems, to)
+
+        @pl.when(to == self.me)
+        def keep():
+            target[to] = source[to]
+
+    def send_all(self, source, target, sems):
+        for step in range(1, 8):
+            self.send(source, target, sems, self.other(step))
+        target[self.me] = source[self.me]
+
+    def received(self, target, sems):
+        for step in range(1, 8):
+            j = self.other(step)
+            self.copy(target.at[j], target.at[j], sems, j, j, j).wait_recv()
+
+    def sent(self, source, sems):
+        for step in range(1, 8):
+            j = self.other(step)
+            self.copy(source.at[j], source.at[j], sems, j, j, j).wait_send()
+
+
+def mask_columns(notes, neg):
+    for j in range(8):
+        neg[j * TOKENS : (j + 1) * TOKENS] = jnp.broadcast_to(notes[j, 0:1], (TOKENS, TOKENS)).T
+
+
+def attend_kernel(give, packed, notes, *refs):
+    if give:
+        pred, o_out, held, stats, turned, pred_out = refs[:6]
+        refs = refs[6:]
+    else:
+        o_out, held, stats, turned = refs[:4]
+        refs = refs[4:]
+    neg, query_side, key_side, message, in_sems, out_sems, swap_local, swap_send, swap_recv = refs
+    plane = Plane()
+    swap = Swap(swap_local, swap_send, swap_recv)
+    if give:
+        greet_all(plane, swap)
+        swap.start(pred, pred_out)
+    else:
+        meet(plane.others())
+    plane.send_all(packed, held, in_sems)
+    mask_columns(notes, neg)
+    stats[...] = jnp.zeros_like(stats)
+    plane.received(held, in_sems)
+    both = held[...].reshape(SEQ_ALL, 3 * PAIR)
+    queries = both[:, :PAIR].astype(FULL)
+    keys = both[:, PAIR : 2 * PAIR].astype(FULL)
+    values_t = both[:, 2 * PAIR :].astype(FULL).T.astype(LOW)
+    for head in range(2):
+        q_side, k_side, unused = head_sides(queries, keys, neg[...], head)
+        query_side[head] = q_side.astype(LOW)
+        key_side[head] = k_side.astype(LOW)
+
+    def chunk(step, carry):
+        at = lax.rem(step + lax.div(plane.me, 2), 4)
+        first = pl.multiple_of(at * BS, BS)
+        for head in range(2):
+            scores = dot_t(key_side[head], query_side[head, pl.ds(first, BS)])
+            most = jnp.max(scores, axis=0, keepdims=True)
+            expos = jnp.exp(scores - most)
+            sums = jnp.sum(expos, axis=0, keepdims=True)
+            part = dot(values_t[head * HD : (head + 1) * HD], expos.astype(LOW)) / sums
+            turned[at, head * HD : (head + 1) * HD] = part
+            stats[head : head + 1, pl.ds(first, BS)] = most + jnp.log(sums)
+        for half in range(2):
+            to = 2 * at + half
+            message[to] = turned[at, :, half * TOKENS : (half + 1) * TOKENS].T.astype(LOW)
+            plane.send_or_keep(message, o_out, out_sems, to)
+        return carry
+
+    lax.fori_loop(0, SEQ_ALL // BS, chunk, 0)
+    plane.received(o_out, out_sems)
+    plane.sent(packed, in_sems)
+    plane.sent(message, out_sems)
+    if give:
+        swap.finish()
+
+
+def greet_all(plane, swap):
+    barrier = pltpu.get_barrier_semaphore()
+    for device in plane.others():
+        pl.semaphore_signal(barrier, inc=1, device_id=device, device_id_type=MESH)
+
+    @pl.when(jnp.logical_not(swap.stays))
+    def partner():
+        pl.semaphore_signal(barrier, inc=1, device_id=swap.to, device_id_type=MESH)
+
+    pl.semaphore_wait(barrier, 7 + jnp.where(swap.stays, 0, 1))
+
+
+def swap_sems(count):
+    return [pltpu.SemaphoreType.DMA((count,))] * 3
+
+
+def attend(packed, notes, pred, collective, name):
+    give = pred is not None
+    return pl.pallas_call(
+        functools.partial(attend_kernel, give),
+        out_shape=(SHAPES["pair"], SHAPES["packed"], SHAPES["stats"], SHAPES["turned"])
+        + ((SHAPES["pred"],) if give else ()),
+        in_specs=[VMEM_AT] * 2 + ([ANY_AT] if give else []),
+        out_specs=(VMEM_AT,) * 4 + ((ANY_AT,) if give else ()),
+        scratch_shapes=[
+            pltpu.VMEM((SEQ_ALL, PAIR), FULL),
+            pltpu.VMEM((2, SEQ_ALL, PAIR), LOW),
+            pltpu.VMEM((2, SEQ_ALL, PAIR), LOW),
+            pltpu.VMEM((8, TOKENS, PAIR), LOW),
+            pltpu.SemaphoreType.DMA((2, 8)),
+            pltpu.SemaphoreType.DMA((2, 8)),
+        ]
+        + swap_sems(1),
+        compiler_params=pltpu.CompilerParams(
+            collective_id=collective, has_side_effects=True, vmem_limit_bytes=VMEM_ASK
+        ),
+        cost_estimate=pl.CostEstimate(flops=1 << 30, bytes_accessed=2 << 20, transcendentals=1 << 21),
+        name=name,
+    )(packed, notes, *((pred,) if give else ()))
+
+
+def attend_back_kernel(n_pool, give, do_in, held, notes, stats, turned, *refs):
+    pools, refs = refs[:n_pool], refs[n_pool:]
+    if give:
+        pred, refs = refs[0], refs[1:]
+    dq_out, dkv_out, refs = refs[0], refs[1], refs[2:]
+    pools_out, refs = refs[:n_pool], refs[n_pool:]
+    if give:
+        pred_out, refs = refs[0], refs[1:]
+    (
+        neg, do_held, query_side, query_plain, key_side, do_side, grad_q, dq_message, dkv_message,
+        in_sems, dq_sems, dkv_sems, swap_local, swap_send, swap_recv, pool_sems,
+    ) = refs
+    x, c, z, y = place()
+    plane = Plane()
+    swap = Swap(swap_local, swap_send, swap_recv)
+    sibling = (2 * x + 1 - c, 2 * z + y)
+    if give:
+        greet_all(plane, swap)
+        swap.start(pred, pred_out)
+    else:
+        meet(plane.others())
+    plane.send_all(do_in, do_held, in_sems)
+    pool_copies = [
+        push(pools[at], pools_out[at], pool_sems.at[0, at], pool_sems.at[1, at], sibling) for at in range(n_pool)
+    ]
+    mask_columns(notes, neg)
+    both = held[...].reshape(SEQ_ALL, 3 * PAIR)
+    queries = both[:, :PAIR].astype(FULL)
+    keys = both[:, PAIR : 2 * PAIR].astype(FULL)
+    keys_t = keys.T.astype(LOW)
+    grad_q[...] = jnp.zeros_like(grad_q)
+    for head in range(2):
+        q_side, k_side, own = head_sides(queries, keys, neg[...], head)
+        query_side[head] = q_side.astype(LOW)
+        query_plain[head] = jnp.where(own, q_side, 0.0).astype(LOW)
+        key_side[head] = k_side.astype(LOW)
+    plane.received(do_held, in_sems)
+    grads = do_held[...].reshape(SEQ_ALL, PAIR).astype(FULL)
+    inner = []
+    for head in range(2):
+        lane = lax.broadcasted_iota(jnp.int32, grads.shape, 1)
+        own = (lane < HD) if head == 0 else (lane >= HD)
+        do_side[head] = jnp.where(own, grads, 0.0).astype(LOW)
+    grads_t = grads.T
+    for head in range(2):
+        side = slice(head * HD, (head + 1) * HD)
+        inner.append(
+            jnp.concatenate(
+                [
+                    jnp.sum(turned[at, side] * grads_t[side, at * BS : (at + 1) * BS], axis=0, keepdims=True)
+                    for at in range(SEQ_ALL // BS)
+                ],
+                axis=1,
+            )
+        )
+    left = lax.broadcasted_iota(jnp.int32, (BS, PAIR), 1) < HD
+    keys_held = [keys_t[head * HD : (head + 1) * HD] for head in range(2)]
+
+    def chunk(at, keys_slice):
+        first = at * BS
+        grad_k = []
+        grad_v = None
+        values = held[2 * at : 2 * at + 2, :, 2 * PAIR :].reshape(BS, PAIR)
+        for head in range(2):
+            scores = dot_t(key_side[head, first : first + BS], query_side[head])
+            probs = jnp.exp(scores - stats[head : head + 1])
+            dprobs = dot_t(values, do_side[head])
+            dscores = (probs * (dprobs - inner[head])).astype(LOW)
+            term = dot(probs.astype(LOW), do_side[head])
+            grad_v = term if grad_v is None else grad_v + term
+            grad_k.append(dot(dscores, query_plain[head]))
+            grad_q[head * HD : (head + 1) * HD] += dot(keys_slice[head], dscores)
+        grad_k = jnp.where(left, grad_k[0], grad_k[1]).astype(LOW)
+        grad_v = grad_v.astype(LOW)
+        for half in range(2):
+            to = 2 * at + half
+            rows = slice(half * TOKENS, (half + 1) * TOKENS)
+            dkv_message[to, :, :PAIR] = grad_k[rows]
+            dkv_message[to, :, PAIR:] = grad_v[rows]
+            plane.send_or_keep(dkv_message, dkv_out, dkv_sems, to)
+
+    for at in range(SEQ_ALL // BS):
+        chunk(at, [part[:, at * BS : (at + 1) * BS] for part in keys_held])
+    for j in range(8):
+        dq_message[j] = (grad_q[:, j * TOKENS : (j + 1) * TOKENS].T * HD**-0.5).astype(LOW)
+        plane.send_or_keep(dq_message, dq_out, dq_sems, j)
+    plane.received(dkv_out, dkv_sems)
+    plane.received(dq_out, dq_sems)
+    plane.sent(do_in, in_sems)
+    plane.sent(dkv_message, dkv_sems)
+    plane.sent(dq_message, dq_sems)
+    for copy in pool_copies:
+        copy.wait()
+    if give:
+        swap.finish()
+
+
+def attend_back(do, held, notes, stats, turned, pools, pred, collective, name):
+    give = pred is not None
+    pools = list(pools)
+    return pl.pallas_call(
+        functools.partial(attend_back_kernel, len(pools), give),
+        out_shape=(SHAPES["pair"], SHAPES["double"])
+        + tuple(shape(pool.shape) for pool in pools)
+        + ((SHAPES["pred"],) if give else ()),
+        in_specs=[VMEM_AT] * 5 + [ANY_AT] * (len(pools) + (1 if give else 0)),
+        out_specs=(VMEM_AT,) * 2 + (ANY_AT,) * (len(pools) + (1 if give else 0)),
+        scratch_shapes=[
+            pltpu.VMEM((SEQ_ALL, PAIR), FULL),
+            pltpu.VMEM((8, TOKENS, PAIR), LOW),
+            pltpu.VMEM((2, SEQ_ALL, PAIR), LOW),
+            pltpu.VMEM((2, SEQ_ALL, PAIR), LOW),
+            pltpu.VMEM((2, SEQ_ALL, PAIR), LOW),
+            pltpu.VMEM((2, SEQ_ALL, PAIR), LOW),
+            pltpu.VMEM((PAIR, SEQ_ALL), FULL),
+            pltpu.VMEM((8, TOKENS, PAIR), LOW),
+            pltpu.VMEM((8, TOKENS, 2 * PAIR), LOW),
+            pltpu.SemaphoreType.DMA((2, 8)),
+            pltpu.SemaphoreType.DMA((2, 8)),
+            pltpu.SemaphoreType.DMA((2, 8)),
+        ]
+        + swap_sems(1)
+        + [pltpu.SemaphoreType.DMA((2, max(1, len(pools))))],
+        compiler_params=pltpu.CompilerParams(
+            collective_id=collective, has_side_effects=True, vmem_limit_bytes=VMEM_ASK
+        ),
+        cost_estimate=pl.CostEstimate(flops=1 << 31, bytes_accessed=2 << 20, transcendentals=1 << 21),
+        name=name,
+    )(do, held, notes, stats, turned, *pools, *((pred,) if give else ()))
+
+
+LEFTS = (WIDE, WIDE, WIDE, DEEP)
+RIGHTS = (3 * WIDE, WIDE, DEEP, WIDE)
+LEFT_AT = (0, WIDE, 2 * WIDE, 3 * WIDE)
+RIGHT_AT = (0, 3 * WIDE, 4 * WIDE, 4 * WIDE + DEEP)
+N_LEFT = 3 * WIDE + DEEP
+N_RIGHT = 5 * WIDE + DEEP
+
+
+def pools_of(block):
+    left = jnp.zeros_like(block)
+    right = jnp.zeros_like(block)
+    for at, base in enumerate((QKV_AT, OUT_AT, UP_AT, DOWN_AT)):
+        inside = block >= base
+        cols = RIGHTS[at]
+        left = jnp.where(inside, LEFT_AT[at] + (block - base) // cols, left)
+        right = jnp.where(inside, RIGHT_AT[at] + (block - base) % cols, right)
+    return left, right
+
+
+def reduce_kernel(left_ids, right_ids, rows_in, *refs):
+    lefts, rights, other_lefts, other_rights = refs[:8], refs[8:16], refs[16:24], refs[24:31]
+    own_out, rows_out = refs[31:33]
+    left_t, right_pool = refs[33:35]
+    x_stage, x_land, yb_stage, yb_land, ym_stage, ym_land = refs[35:41]
+    zb_stage, zb_land, zm_stage, zm_land, both_stage, both_land = refs[41:47]
+    pair_rows, chip_rows, plane_rows, row_land, row_z = refs[47:52]
+    pool_sems, pool_send, pool_recv, send_sems, recv_sems, row_send, row_recv = refs[52:59]
+    x, c, z, y = place()
+    samp = 2 * x + c
+    blk = 2 * z + y
+    to_c = (2 * x + 1 - c, blk)
+    to_x = (2 * (1 - x) + c, blk)
+    to_y = (samp, 2 * z + 1 - y)
+    to_z = [(samp, 2 * lax.rem(z + step, 4) + y) for step in (1, 2, 3)]
+    meet_all()
+    first = pl.ds(RIGHT_AT[0], RIGHTS[0])
+    dqkv_copy = push(
+        rights[0], right_pool.at[first, pl.ds(2 * TOKENS, TOKENS)], pool_send.at[0], pool_recv.at[0], to_c
+    )
+    row_copy = push(rows_in, row_land.at[0], row_send.at[0], row_recv.at[0], to_c)
+    here = []
+
+    def load(part, layer, kind, left):
+        counts, bases = (LEFTS, LEFT_AT) if left else (RIGHTS, RIGHT_AT)
+        ids = pl.ds(bases[kind], counts[kind])
+        tokens = pl.ds(layer * TOKENS, TOKENS)
+        target = left_t.at[ids, :, tokens] if left else right_pool.at[ids, tokens]
+        here.append(pltpu.make_async_copy(part, target, pool_sems.at[len(here)]))
+        here[-1].start()
+
+    for at in range(8):
+        layer, kind = divmod(at, 4)
+        load(lefts[at], layer, kind, True)
+        load(other_lefts[at], 2 + layer, kind, True)
+        load(rights[at], layer, kind, False)
+        if at > 0:
+            load(other_rights[at - 1], 2 + layer, kind, False)
+    row_copy.wait_recv()
+    pair_rows[...] = rows_in[...] + row_land[0]
+    row_copies = [row_copy, push(pair_rows, row_land.at[1], row_send.at[1], row_recv.at[1], to_x)]
+    for copy in here:
+        copy.wait()
+    dqkv_copy.wait_recv()
+
+    def group(half, k):
+        return 2 * lax.rem(z + 1 + k, 4) + (1 - y if half == 0 else y)
+
+    def part(half, k, offset):
+        slot = group(half, k) * GROUP + c * HALF + offset
+        return [dot(left_t[left_ids[slot + i]], right_pool[right_ids[slot + i]]) for i in range(QUART)]
+
+    mine, other, both = x * 8, (1 - x) * 8, QUART
+
+    def link(kind, k, stage, land, to):
+        return pltpu.make_async_remote_copy(
+            src_ref=stage, dst_ref=land, send_sem=send_sems.at[kind, k], recv_sem=recv_sems.at[kind, k],
+            device_id=to, device_id_type=MESH,
+        )
+
+    def along_x(half, k):
+        return link(half, k, x_stage.at[half, k], x_land.at[half, k], to_x)
+
+    def along_y_both(k):
+        return link(2, k, yb_stage.at[k], yb_land.at[k], to_y)
+
+    def along_y_mine(k):
+        return link(3, k, ym_stage.at[k], ym_land.at[k], to_y)
+
+    def along_z_both(k):
+        return link(4, k, zb_stage.at[k], zb_land.at[k], (samp, group(1, k)))
+
+    def along_z_mine(k):
+        return link(5, k, zm_stage.at[k], zm_land.at[k], (samp, group(1, k)))
+
+    def begin(k, carry):
+        for i, value in enumerate(part(0, k, both)):
+            yb_stage[k, i] = value.astype(LOW)
+        along_y_both(k).start()
+        for i, value in enumerate(part(0, k, other)):
+            x_stage[0, k, i] = value.astype(LOW)
+        along_x(0, k).start()
+        return carry
+
+    lax.fori_loop(0, 4, begin, 0)
+
+    def more(k, carry):
+        for i, value in enumerate(part(1, k, other)):
+            x_stage[1, k, i] = value.astype(LOW)
+        along_x(1, k).start()
+        return carry
+
+    lax.fori_loop(0, 4, more, 0)
+
+    def middle(k, carry):
+        values = part(0, k, mine)
+        along_x(0, k).wait_recv()
+        for i, value in enumerate(values):
+            ym_stage[k, i] = (value + x_land[0, k, i].astype(FULL)).astype(LOW)
+        along_y_mine(k).start()
+        values = part(1, k, both)
+        along_y_both(k).wait_recv()
+        for i, value in enumerate(values):
+            zb_stage[k, i] = (value + yb_land[k, i].astype(FULL)).astype(LOW)
+
+        @pl.when(k < 3)
+        def send_on():
+            along_z_both(k).start()
+
+        return carry
+
+    lax.fori_loop(0, 4, middle, 0)
+    row_copies[1].wait_recv()
+    chip_rows[...] = pair_rows[...] + row_land[1]
+    row_copies.append(push(chip_rows, row_land.at[2], row_send.at[2], row_recv.at[2], to_y))
+
+    def late(k, carry):
+        values = part(1, k, mine)
+        along_x(1, k).wait_recv()
+        values = [value + x_land[1, k, i].astype(FULL) for i, value in enumerate(values)]
+        along_y_mine(k).wait_recv()
+        for i, value in enumerate(values):
+            zm_stage[k, i] = (value + ym_land[k, i].astype(FULL)).astype(LOW)
+
+        @pl.when(k < 3)
+        def send_on():
+            along_z_mine(k).start()
+
+        return carry
+
+    lax.fori_loop(0, 4, late, 0)
+    row_copies[2].wait_recv()
+    plane_rows[...] = chip_rows[...] + row_land[2]
+    for step in range(3):
+        row_copies.append(
+            push(plane_rows, row_z.at[z], row_send.at[3 + step], row_recv.at[3 + step], to_z[step])
+        )
+    row_z[z] = plane_rows[...]
+    for k in range(3):
+        along_z_both(k).wait_recv()
+    for i in range(QUART):
+        value = zb_stage[3, i].astype(FULL)
+        for k in range(3):
+            value = value + zb_land[k, i].astype(FULL)
+        both_stage[i // 2, i % 2] = value.astype(LOW)
+    last = link(6, 0, both_stage.at[1 - x], both_land, to_x)
+    last.start()
+    for k in range(3):
+        along_z_mine(k).wait_recv()
+    for i in range(QUART):
+        value = zm_stage[3, i].astype(FULL)
+        for k in range(3):
+            value = value + zm_land[k, i].astype(FULL)
+        own_out[i] = value.astype(LOW)
+    last.wait_recv()
+    for i in range(2):
+        own_out[QUART + i] = (both_stage[x, i].astype(FULL) + both_land[i].astype(FULL)).astype(LOW)
+    for step in range(3):
+        row_copies[3 + step].wait_recv()
+    rows_out[...] = (row_z[0] + row_z[1]) + (row_z[2] + row_z[3])
+    for copy in [dqkv_copy] + row_copies + [last]:
+        copy.wait_send()
+
+    def drain(k, carry):
+        along_x(0, k).wait_send()
+        along_x(1, k).wait_send()
+        along_y_both(k).wait_send()
+        along_y_mine(k).wait_send()
+
+        @pl.when(k < 3)
+        def sent_on():
+            along_z_both(k).wait_send()
+            along_z_mine(k).wait_send()
+
+        return carry
+
+    lax.fori_loop(0, 4, drain, 0)
+
+
+def blocks_of(*lead):
+    return pltpu.VMEM(lead + (BS, BS), LOW)
+
+
+def reduce_grads(left_ids, right_ids, rows, lefts, rights, others):
+    return pl.pallas_call(
+        reduce_kernel,
+        out_shape=(shape((6, BS, BS)), SHAPES["rows"]),
+        in_specs=[SMEM_IN] * 2 + [VMEM_AT] + [ANY_AT] * 31,
+        out_specs=(VMEM_AT, VMEM_AT),
+        scratch_shapes=[
+            pltpu.VMEM((N_LEFT, BS, 4 * TOKENS), LOW),
+            pltpu.VMEM((N_RIGHT, 4 * TOKENS, BS), LOW),
+            blocks_of(2, 4, QUART),
+            blocks_of(2, 4, QUART),
+            blocks_of(4, QUART),
+            blocks_of(4, QUART),
+            blocks_of(4, QUART),
+            blocks_of(4, QUART),
+            blocks_of(4, QUART),
+            blocks_of(3, QUART),
+            blocks_of(4, QUART),
+            blocks_of(3, QUART),
+            blocks_of(2, 2),
+            blocks_of(2),
+            pltpu.VMEM((20, D), FULL),
+            pltpu.VMEM((20, D), FULL),
+            pltpu.VMEM((20, D), FULL),
+            pltpu.VMEM((3, 20, D), FULL),
+            pltpu.VMEM((4, 20, D), FULL),
+            pltpu.SemaphoreType.DMA((31,)),
+            pltpu.SemaphoreType.DMA((1,)),
+            pltpu.SemaphoreType.DMA((1,)),
+            pltpu.SemaphoreType.DMA((7, 4)),
+            pltpu.SemaphoreType.DMA((7, 4)),
+            pltpu.SemaphoreType.DMA((6,)),
+            pltpu.SemaphoreType.DMA((6,)),
+        ],
+        compiler_params=pltpu.CompilerParams(
+            collective_id=5, has_side_effects=True, vmem_limit_bytes=VMEM_ASK
+        ),
+        cost_estimate=pl.CostEstimate(flops=6 << 30, bytes_accessed=40 << 20, transcendentals=0),
+        name="reduce_grads",
+    )(left_ids, right_ids, rows, *lefts, *rights, *others)
+
+
+def halves(value):
+    high = value.astype(LOW)
+    return high, (value - high.astype(FULL)).astype(LOW)
+
+
+def fine(left, right):
+    return dot(
+        jnp.concatenate([left[0], left[1], left[0]], axis=1),
+        jnp.concatenate([right[0], right[0], right[1]], axis=0),
+    )
+
+
+def statistic(gram, shrink, diag, eye):
+    return jnp.where(eye, 0.5 * diag, 0.0) + shrink * gram
+
+
+def roots(stats, eye):
+    scales = [jnp.sqrt(jnp.sum(jnp.sum(stat * stat, axis=1, keepdims=True), axis=0, keepdims=True)) for stat in stats]
+    moving = [stat / scale for stat, scale in zip(stats, scales)]
+    approx = [None] * len(stats)
+    ahead = range(len(stats))
+    for iteration in range(ITERS):
+        factors = [(jnp.where(eye, 5.0, 0.0) - moving[i]) * 0.25 for i in ahead]
+        parts = [halves(factor) for factor in factors]
+        if iteration == 0:
+            approx = [factors[i] * lax.rsqrt(jnp.sqrt(scales[i])) for i in ahead]
+        else:
+            approx = [fine(halves(approx[i]), parts[i]) for i in ahead]
+        if iteration < ITERS - 1:
+            squares = [halves(fine(parts[i], parts[i])) for i in ahead]
+            fourths = [halves(fine(squares[i], squares[i])) for i in ahead]
+            moving = [fine(fourths[i], halves(moving[i])) for i in ahead]
+    return approx
+
+
+def shampoo_kernel(
+    own, left_diag, right_diag, grad_in, grads_out, moves_out, grad_out, staged, local_sems, send_sems, recv_sems,
+    swap_local, swap_send, swap_recv,
+):
+    x, c, z, y = place()
+    blk = 2 * z + y
+    to_c = (2 * x + 1 - c, blk)
+    to_x = (2 * (1 - x) + c, blk)
+    meet_all()
+    swap = Swap(swap_local, swap_send, swap_recv)
+    swap.start(grad_in, grad_out)
+    mine = c * HALF + x * 8
+    both = c * HALF + QUART + 2 * x
+    far_mine = c * HALF + (1 - x) * 8
+    far_both = c * HALF + QUART + 2 * (1 - x)
+
+    def link(kind, k, src, dst, to):
+        return pltpu.make_async_remote_copy(
+            src_ref=src, dst_ref=dst, send_sem=send_sems.at[kind, k], recv_sem=recv_sems.at[kind, k],
+            device_id=to, device_id_type=MESH,
+        )
+
+    def grad_copy(kind, at, to):
+        if at == 0:
+            return link(kind, at, own.at[pl.ds(0, QUART)], grads_out.at[pl.ds(mine, QUART)], to)
+        return link(kind, at, own.at[pl.ds(QUART, 2)], grads_out.at[pl.ds(both, 2)], to)
+
+    def grad_on(at):
+        where = grads_out.at[pl.ds(far_mine, QUART)] if at == 0 else grads_out.at[pl.ds(far_both, 2)]
+        return link(2, at, where, where, to_c)
+
+    grad_copies = [grad_copy(kind, at, to) for kind, to in ((0, to_x), (1, to_c)) for at in (0, 1)]
+    for copy in grad_copies:
+        copy.start()
+    local = [
+        pltpu.make_async_copy(own.at[pl.ds(0, QUART)], grads_out.at[pl.ds(mine, QUART)], local_sems.at[0]),
+        pltpu.make_async_copy(own.at[pl.ds(QUART, 2)], grads_out.at[pl.ds(both, 2)], local_sems.at[1]),
+    ]
+    for copy in local:
+        copy.start()
+    eye = lax.broadcasted_iota(jnp.int32, (BS, BS), 0) == lax.broadcasted_iota(jnp.int32, (BS, BS), 1)
+
+    def slot_of(i, far=False):
+        first = (far_mine if far else mine) + i
+        second = (far_both if far else both) + i - QUART
+        return jnp.where(i < QUART, first, second)
+
+    def move_copy(kind, i, to):
+        return link(kind, i, staged.at[i], moves_out.at[slot_of(i)], to)
+
+    def move_on(i):
+        where = moves_out.at[slot_of(i, True)]
+        return link(5, i, where, where, to_c)
+
+    def kept(i):
+        return pltpu.make_async_copy(staged.at[i], moves_out.at[slot_of(i)], local_sems.at[2 + i])
+
+    def pair(at, carry):
+        held = []
+        stats = []
+        for i in (2 * at, 2 * at + 1):
+            low = own[i]
+            grad = low.astype(FULL)
+            mean = jnp.sum(jnp.sum(grad * grad, axis=1, keepdims=True), axis=0, keepdims=True) / (BS * BS)
+            shrink = 0.5 / (mean + 1e-06)
+            low_t = grad.T.astype(LOW)
+            slot = slot_of(i)
+            stats.append(statistic(dot(low, low_t), shrink, left_diag[pl.ds(slot, 1)], eye))
+            stats.append(statistic(dot(low_t, low), shrink, right_diag[pl.ds(slot, 1)], eye))
+            held.append((i, low, lax.rsqrt(mean + 1e-06)))
+        sides = roots(stats, eye)
+        for n, (i, low, rate) in enumerate(held):
+            high, rest = halves(sides[2 * n])
+            turned = dot(jnp.concatenate([high, rest], axis=1), jnp.concatenate([low, low], axis=0)) * rate
+            staged[i] = fine(halves(turned), halves(sides[2 * n + 1])).astype(LOW)
+            move_copy(3, i, to_x).start()
+            move_copy(4, i, to_c).start()
+            kept(i).start()
+        return carry
+
+    lax.fori_loop(0, 3, pair, 0)
+    for at in (0, 1):
+        grad_copies[at].wait_recv()
+        grad_on(at).start()
+
+    def pass_on(i, carry):
+        move_copy(3, i, to_x).wait_recv()
+        move_on(i).start()
+        return carry
+
+    lax.fori_loop(0, 6, pass_on, 0)
+    for at in (0, 1):
+        grad_copies[2 + at].wait_recv()
+        grad_on(at).wait_recv()
+        grad_on(at).wait_send()
+        local[at].wait()
+    for copy in grad_copies:
+        copy.wait_send()
+
+    def drain(i, carry):
+        move_copy(4, i, to_c).wait_recv()
+        move_on(i).wait_recv()
+        move_copy(3, i, to_x).wait_send()
+        move_copy(4, i, to_c).wait_send()
+        move_on(i).wait_send()
+        kept(i).wait()
+        return carry
+
+    lax.fori_loop(0, 6, drain, 0)
+    swap.finish()
+
+
+def shampoo(own, left_start, right_start, grad):
+    return pl.pallas_call(
+        shampoo_kernel,
+        out_shape=(shape((GROUP, BS, BS)), shape((GROUP, BS, BS)), SHAPES["pred"]),
+        in_specs=[VMEM_AT] * 3 + [ANY_AT],
+        out_specs=(ANY_AT,) * 3,
+        scratch_shapes=[
+            blocks_of(6),
+            pltpu.SemaphoreType.DMA((8,)),
+            pltpu.SemaphoreType.DMA((6, 6)),
+            pltpu.SemaphoreType.DMA((6, 6)),
+        ]
+        + swap_sems(1),
+        compiler_params=pltpu.CompilerParams(
+            collective_id=6, has_side_effects=True, vmem_limit_bytes=VMEM_ASK
+        ),
+        cost_estimate=pl.CostEstimate(flops=30 << 30, bytes_accessed=10 << 20, transcendentals=0),
+        name="shampoo",
+    )(own, left_start, right_start, grad)
+
+
+def finish_kernel(grad, move, weight, left_diag, right_diag, grad_out, left_out, right_out, new_out, low_out):
+    eye = lax.broadcasted_iota(jnp.int32, (BS, BS), 0) == lax.broadcasted_iota(jnp.int32, (BS, BS), 1)
+
+    def mean(value):
+        return jnp.sum(jnp.sum(value, axis=1, keepdims=True), axis=0, keepdims=True) / (BS * BS)
+
+    for i in range(STEP):
+        low = grad[i]
+        full = low.astype(FULL)
+        grad_out[i] = full
+        shrink = 0.5 / (mean(full * full) + 1e-06)
+        low_t = full.T.astype(LOW)
+        left_out[i] = statistic(dot(low, low_t), shrink, left_diag[i], eye)
+        right_out[i] = statistic(dot(low_t, low), shrink, right_diag[i], eye)
+        step = move[i].astype(FULL)
+        start = weight[i]
+        ratio = jnp.sqrt(mean(start * start)) * lax.rsqrt(mean(step * step) + 1e-06)
+        new = start - step_rate * ratio * step
+        new_out[i] = new
+        low_out[i] = new.astype(LOW)
+
+
+STEP = 4
+
+
+def finish_slots(grads, moves, masters, left_start, right_start):
+    block = pl.BlockSpec((STEP, BS, BS), lambda i: (i, 0, 0))
+    row = pl.BlockSpec((STEP, 1, BS), lambda i: (i, 0, 0))
+    return pl.pallas_call(
+        finish_kernel,
+        grid=(GROUP // STEP,),
+        compiler_params=pltpu.CompilerParams(vmem_limit_bytes=VMEM_ASK),
+        out_shape=tuple(shape((GROUP, BS, BS), kind) for kind in (FULL, FULL, FULL, FULL, LOW)),
+        in_specs=[block, block, block, row, row],
+        out_specs=(block,) * 5,
+        cost_estimate=pl.CostEstimate(flops=2 << 30, bytes_accessed=39 << 20, transcendentals=0),
+        name="finish_slots",
+    )(grads, moves, masters, left_start.reshape(GROUP, 1, BS), right_start.reshape(GROUP, 1, BS))
+
+
+def layers(inputs, cot_first, cot_second, slots, leads, vectors, copies, notes):
+    act_held = pltpu.VMEM((DEEP, TOKENS, BS), LOW)
+    hidden_one, a_one, packed = plain(
+        first_kernel, [SMEM_IN] * 2 + [VMEM_AT] * 2 + [ANY_AT], ("wide", "four_t", "packed"), ("qkv",), 1 << 30, "first"
+    )(slots, leads, inputs, vectors, copies)
+    o_msg, held_one, stats_one, turned_one, cot_second = attend(packed, notes, cot_second, 1, "attend_one")
+    mid_one, u_one, o_one, n_one, act_one, pred_one, hidden_two, a_two, packed = plain(
+        between_kernel,
+        [SMEM_IN] * 2 + [VMEM_AT] * 3 + [ANY_AT],
+        ("wide", "up", "four_t", "four_t", "sixteen_t", "pred", "wide", "four_t", "packed"),
+        ("out", "up", "down", "qkv"),
+        3 << 30,
+        "between",
+        [act_held],
+    )(slots, leads, hidden_one, o_msg, vectors, copies)
+    o_msg, held_two, stats_two, turned_two, cot_first = attend(packed, notes, cot_first, 1, "attend_two")
+    o_two, n_two, act_two, pred_two, du_two, dz1_two, dz2_two, do_msg, dm_two, rows = plain(
+        turn_kernel,
+        [SMEM_IN] + [VMEM_AT] * 4 + [ANY_AT],
+        ("four_t", "four_t", "sixteen_t", "pred", "sixteen", "four", "four", "pair", "wide", "rows"),
+        ("out", "up", "down"),
+        5 << 30,
+        "turn",
+        [pltpu.VMEM((DEEP, TOKENS, BS), FULL), act_held],
+    )(slots, hidden_two, o_msg, cot_second, vectors, copies)
+    dq_msg, dkv_msg, pred_one = attend_back(
+        do_msg, held_two, notes, stats_two, turned_two, (), pred_one, 3, "attend_back_two"
+    )
+    dqkv_two, du_one, dz1_one, dz2_one, do_msg, dm_one, rows = plain(
+        back_between_kernel,
+        [SMEM_IN] * 2 + [VMEM_AT] * 9 + [ANY_AT],
+        ("twelve", "sixteen", "four", "four", "pair", "wide", "rows"),
+        ("out", "up", "down", "qkv"),
+        3 << 30,
+        "back_between",
+    )(slots, leads, dm_two, hidden_two, dq_msg, dkv_msg, rows, cot_first, mid_one, u_one, vectors, copies)
+    lefts = (a_one, o_one, n_one, act_one, a_two, o_two, n_two, act_two)
+    rights = (dz1_one, du_one, dz2_one, dqkv_two, dz1_two, du_two, dz2_two)
+    dq_msg, dkv_msg, *others, pred_two = attend_back(
+        do_msg, held_one, notes, stats_one, turned_one, lefts + rights, pred_two, 4, "attend_back_one"
+    )
+    dqkv_one, input_grad, rows = plain(
+        last_kernel,
+        [SMEM_IN] * 2 + [VMEM_AT] * 6 + [ANY_AT],
+        ("twelve", "pred", "rows"),
+        ("qkv",),
+        1 << 30,
+        "last",
+    )(slots, leads, dm_one, hidden_one, dq_msg, dkv_msg, rows, vectors, copies)
+    return pred_one, pred_two, input_grad, lefts, (dqkv_one,) + rights, others, rows
+
+
+def local_tuned(
+    inputs,
+    cot_first,
+    cot_second,
+    valid_flags,
+    lead_steps,
+    masters,
+    assignment,
+    left_start,
+    right_start,
+    vectors,
+    vec_moment,
+):
+    notes = jnp.concatenate(
+        [
+            valid_flags.astype(FULL) - 1.0,
+            jnp.pad(lead_steps.astype(FULL).T, ((0, 0), (0, TOKENS - 2))),
+            jnp.zeros((6, TOKENS), FULL),
+        ],
+        axis=0,
+    )
+    copies, notes, rows_in = gather_weights(masters, notes, inputs)
+    leads = notes[0, 1, :2].astype(jnp.int32).reshape(2, 1)
+    pred_one, pred_two, input_grad, lefts, rights, others, rows = layers(
+        rows_in, cot_first, cot_second, assignment, leads, vectors, copies, notes
+    )
+    position = jnp.arange(NB, dtype=jnp.int32)
+    inverse = jnp.sum(
+        jnp.where(assignment[None, :] == position[:, None], position[None, :], 0), axis=1
+    )
+    left_ids, right_ids = pools_of(inverse)
+    own, vec_grads = reduce_grads(left_ids, right_ids, rows, lefts, rights, others)
+    grads, moves, input_grad = shampoo(own, left_start, right_start, input_grad)
+    input_grad = input_grad.astype(FULL)
+    matrix_grads, left_stats, right_stats, new_masters, new_copies = finish_slots(
+        grads, moves, masters, left_start, right_start
+    )
+    scaled_vec = vec_grads * lax.rsqrt(
+        jnp.mean(vec_grads * vec_grads, axis=1, keepdims=True) + 1e-06
+    )
+    vec_moments = 0.5 * vec_moment + 0.5 * scaled_vec * scaled_vec
+    new_vectors = vectors - vector_rate * scaled_vec * lax.rsqrt(vec_moments)
+    return (
+        pred_one,
+        pred_two,
+        input_grad,
+        matrix_grads,
+        left_stats,
+        right_stats,
+        new_masters,
+        new_copies,
+        vec_grads,
+        vec_moments,
+        new_vectors,
+    )
+
+
 def solution(mesh):
     placed = (
         P("samp", "blk", None),
@@ -480,8 +2077,9 @@
         P(),
         P(),
     )
+    fits = mesh.shape["samp"] == 4 and mesh.shape["blk"] == 8
     return jax.shard_map(
-        local,
+        local_tuned if fits else local_any,
         mesh=mesh,
         in_specs=placed,
         out_specs=(

time: 2780 us -> 496 us (0.18)
  waiting for transfers between devices: 1560 us -> 0 us
  matrix products: 619 us -> 0 us
  Pallas kernels: 0 us -> 476 us
  local copies, waits for them, and re-layouts: 316 us -> 4.06 us
  other arithmetic: 134 us -> 6.04 us
  blocking collectives: 117 us -> 0 us
    reduce_scatter x1 -> x0, waiting for transfers between devices: 799 us -> none  [local(): shared = lax.psum_scatter(slotted, 'blk', scatter_dimension=0, tiled=True)]
    dot_general x84 -> x0, matrix products: 619 us -> none  [the longest x12 128 us: invert_root(): approx = jnp.dot(approx, factor, precision=HIGH)]
    all_gather x9 -> x0, waiting for transfers between devices: 583 us -> none  [the longest x1 479 us: local(): lax.all_gather(masters.astype(jnp.bfloat16), 'blk', axis=0, tiled=True)]
    pallas_call x0 -> x13, Pallas kernels: none -> 476 us  [the longest x1 126 us: reduce_grads(): pl.pallas_call(reduce_kernel, out_shape=(shape((6, BS, BS)), SHAPES['rows...]
    psum x2 -> x0, waiting for transfers between devices: 180 us -> none  [the longest x1 111 us: local(): vec_grads = lax.psum(vec_one + vec_two, ('samp', 'blk'))]
    all_gather x5 -> x0, blocking collectives: 117 us -> none  [the longest x2 50.7 us: backward(): lax.all_gather(inner, 'blk', axis=1, tiled=True)]
    reshape x14 -> x2, local copies, waits for them, and re-layouts: 115 us -> 1.25 us  [the longest x1 0.63 us: finish_slots(): left_start.reshape(GROUP, 1, BS)]
    select_n x4 -> x1, other arithmetic: 55.5 us -> 0.56 us  [pools_of(): right = jnp.where(inside, RIGHT_AT[at] + (block - base) % cols, right)]
  transfers between devices with their start and end apart: 12 -> 0, of which waited for: 9 -> 0; matrix products, arithmetic and copies ran while one was open for 11% -> 0% of each run, Pallas kernels for 0% -> 0%
where the time goes in v1:
time: 496 us; the launch traced here: 488 us
  Pallas kernels  476 us (96%)
  other arithmetic  6.04 us (1%)
    pallas_call x1, Pallas kernels, reduce_grads(): pl.pallas_call(reduce_kernel, out_shape=(shape((6, BS, BS)), SHAPES['rows...  126 us
    pallas_call x1, Pallas kernels, gather_weights(): pl.pallas_call(weights_kernel, out_shape=(jax.ShapeDtypeStruct((NB, BS, B...  111 us
    pallas_call x2, Pallas kernels, attend(): pl.pallas_call(functools.partial(attend_kernel, give), out_shape=(SHAPES[...  59.6 us
    pallas_call x2, Pallas kernels, attend_back(): pl.pallas_call(functools.partial(attend_back_kernel, len(pools), give), o...  51.7 us
    pallas_call x1, Pallas kernels, shampoo(): pl.pallas_call(shampoo_kernel, out_shape=(shape((GROUP, BS, BS)), shape((...  48.7 us
    pallas_call x1, Pallas kernels, layers(): plain(back_between_kernel, [SMEM_IN] * 2 + [VMEM_AT] * 9 + [ANY_AT], ('tw...  20.2 us
    pallas_call x1, Pallas kernels, layers(): plain(turn_kernel, [SMEM_IN] + [VMEM_AT] * 4 + [ANY_AT], ('four_t', 'four...  18.6 us
    pallas_call x1, Pallas kernels, finish_slots(): pl.pallas_call(finish_kernel, grid=(GROUP // STEP,), compiler_params=pltp...  15.1 us

profile of v1, /device:TPU:3, one launch (start us, length us, event | category | flops | bytes accessed | tf_op | source)
XLA Modules:
  0.0 487.6 jit_solution(1053448837016663774)
XLA Ops:
  0.6 0.7 convert_bitcast_fusion.1
  1.3 0.7 convert_add_fusion
  2.0 0.1 pad.7.clone
  2.0 0.7 fusion.1.notes
  2.7 111.1 %gather_weights.1 = (bf16[192,256,256]{2,1,0:T(8,128)(2,1)}, f32[8,8,128]{2,1,0:T(8,128)}, bf16[1,128,1024]{2,1,0:T(8,128)(2,1)}) custom-call(f32[24,256,256]{2,1,0:T(8,128)} %weight.1, f32[8,128]{1,0:T(8,128)} %fusion.1.notes, bf16[1,128,1024]{2,1,0:T(8,128)(2,1)} %rows_in.1), custom_call_target="tpu_custom_call" | custom-call | tf_op jit(solution)/shard_map/gather_weights/pallas_call | solution.py:620
  113.8 0.7 convert_bitcast_fusion
  114.5 0.7 copy.27.leads
  115.2 6.0 %first.1 = (f32[128,1024]{1,0:T(8,128)}, bf16[4,256,128]{2,1,0:T(8,128)(2,1)}, bf16[8,128,384]{2,1,0:T(8,128)(2,1)}) custom-call(s32[192]{0:T(256)} %slots.9, s32[2,1]{1,0:T(2,128)} %copy.27.leads, bf16[1,128,1024]{2,1,0:T(8,128)(2,1)} %get-tuple-element.88.x, f32[20,1024]{1,0:T(8,128)} %vecs.9, bf16[192,256,256]{2,1,0:T(8,128)(2,1)} %get-tuple-element.89.copies), custom_call_target="tpu_custom_call" | custom-call | flops 1073741824 | bytes 25165824 | tf_op jit(solution)/shard_map/first/pallas_call | solution.py:1959
  121.2 29.3 %attend_one.1 = (bf16[8,128,128]{2,1,0:T(8,128)(2,1)}, bf16[8,128,384]{2,1,0:T(8,128)(2,1)}, f32[8,1024]{1,0:T(8,128)}, f32[4,128,256]{2,1,0:T(8,128)}, bf16[1,128,1024]{2,1,0:T(8,128)(2,1)}) custom-call(bf16[8,128,384]{2,1,0:T(8,128)(2,1)} %get-tuple-element.91.packed, f32[8,8,128]{2,1,0:T(8,128)} %get-tuple-element.87.notes, bf16[1,128,1024]{2,1,0:T(8,128)(2,1)} %refs_0_.2), custom_call_target="tpu_custom_call" | custom-call | flops 1073741824 | bytes 2097152 | tf_op jit(solution)/shard_map/attend_one/pallas_call | solution.py:1351
  150.5 12.1 %between.1 = (f32[128,1024]{1,0:T(8,128)}, f32[16,128,256]{2,1,0:T(8,128)}, bf16[4,256,128]{2,1,0:T(8,128)(2,1)}, bf16[4,256,128]{2,1,0:T(8,128)(2,1)}, bf16[16,...) custom-call(s32[192]{0:T(256)} %slots.9, ...), custom_call_target="tpu_custom_call" | custom-call | flops 3221225472 | bytes 25165824 | tf_op jit(solution)/shard_map/between/pallas_call | solution.py:1963
  162.6 30.3 %attend_two.1 = (bf16[8,128,128]{2,1,0:T(8,128)(2,1)}, bf16[8,128,384]{2,1,0:T(8,128)(2,1)}, f32[8,1024]{1,0:T(8,128)}, f32[4,128,256]{2,1,0:T(8,128)}, bf16[1,128,1024]{2,1,0:T(8,128)(2,1)}) custom-call(bf16[8,128,384]{2,1,0:T(8,128)(2,1)} %get-tuple-element.94.packed, f32[8,8,128]{2,1,0:T(8,128)} %get-tuple-element.87.notes, bf16[1,128,1024]{2,1,0:T(8,128)(2,1)} %refs_0_.3), custom_call_target="tpu_custom_call" | custom-call | flops 1073741824 | bytes 2097152 | tf_op jit(solution)/shard_map/attend_two/pallas_call | solution.py:1351
  192.9 18.6 %turn.1 = (bf16[4,256,128]{2,1,0:T(8,128)(2,1)}, bf16[4,256,128]{2,1,0:T(8,128)(2,1)}, bf16[16,256,128]{2,1,0:T(8,128)(2,1)}, bf16[1,128,1024]{2,1,0:T(8,128)(2,...) custom-call(s32[192]{0:T(256)} %slots.9, ...), custom_call_target="tpu_custom_call" | custom-call | flops 5368709120 | bytes 25165824 | tf_op jit(solution)/shard_map/turn/pallas_call | solution.py:1973
  211.5 26.8 %attend_back_two.1 = (bf16[8,128,128]{2,1,0:T(8,128)(2,1)}, bf16[8,128,256]{2,1,0:T(8,128)(2,1)}, bf16[1,128,1024]{2,1,0:T(8,128)(2,1)}) custom-call(bf16[8,128,128]{2,1,0:T(8,128)(2,1)} %get-tuple-element.97.do_in, bf16[8,128,384]{2,1,0:T(8,128)(2,1)} %get-tuple-element.98.held, f32[8,8,128]{2,1,0:T(8,128)} %get-tuple-element.87.notes, ...), custom_call_target="tpu_custom_call" | custom-call | flops 2147483648 | bytes 2097152 | tf_op jit(solution)/shard_map/attend_back_two/pallas_call | solution.py:1474
  238.2 20.2 %back_between.1 = (bf16[12,128,256]{2,1,0:T(8,128)(2,1)}, bf16[16,128,256]{2,1,0:T(8,128)(2,1)}, bf16[4,128,256]{2,1,0:T(8,128)(2,1)}, bf16[4,128,256]{2,1,0:T(8...) custom-call(s32[192]{0:T(256)} %slots.9, s32[2,1]{1,0:T(2,128)} %copy.27.leads, ...), custom_call_target="tpu_custom_call" | custom-call | flops 3221225472 | bytes 25165824 | tf_op jit(solution)/shard_map/back_between/pallas_call | solution.py:1985
  258.5 0.0 copy-start.5
  258.5 25.0 %attend_back_one.1 = (bf16[8,128,128]{2,1,0:T(8,128)(2,1)}, bf16[8,128,256]{2,1,0:T(8,128)(2,1)}, bf16[4,256,128]{2,1,0:T(8,128)(2,1)}, bf16[4,256,128]{2,1,0:T(...) custom-call(bf16[8,128,128]{2,1,0:T(8,128)(2,1)} %get-tuple-element., ...), custom_call_target="tpu_custom_call" | custom-call | flops 2147483648 | bytes 2097152 | tf_op jit(solution)/shard_map/attend_back_one/pallas_call | solution.py:1474
  283.5 0.1 select_reduce_fusion
  283.6 0.6 fusion.4
  284.2 7.6 %last.1 = (bf16[12,128,256]{2,1,0:T(8,128)(2,1)}, bf16[1,128,1024]{2,1,0:T(8,128)(2,1)}, f32[20,1024]{1,0:T(8,128)}) custom-call(s32[192]{0:T(256)} %slots.9, s32[2,1]{1,0:T(2,128)} %copy.27.leads, f32[128,1024]{1,0:T(8,128)} %get-tuple-element.131.dm_in, f32[128,1024]{1,0:T(8,128)} %get-tuple-element.90.h_in, ...), custom_call_target="tpu_custom_call" | custom-call | flops 1073741824 | bytes 25165824 | tf_op jit(solution)/shard_map/last/pallas_call | solution.py:1998
  291.8 125.5 %reduce_grads.1 = (bf16[6,256,256]{2,1,0:T(8,128)(2,1)}, f32[20,1024]{1,0:T(8,128)}) custom-call(s32[192]{0:T(256)} %get-tuple-element.166.left_ids, s32[192]{0:T(256)} %get-tuple-element.165.right_ids, f32[20,1024]{1,0:T(8,128)} %get-tuple-element.135.rows_in, bf16[4,256,128]{2,1,0:T(8,128)(2,1)} %get-tuple-element.114.refs_0_, ...), custom_call_target="tpu_custom_call" | custom-call | flops 6442450944 | bytes 41943040 | tf_op jit(solution)/shard_map/reduce_grads/pallas_call | solution.py:1708
  417.3 0.0 copy-start.6
  417.3 0.0 copy-start.7
  417.3 48.7 %shampoo.1 = (bf16[24,256,256]{2,1,0:T(8,128)(2,1)}, bf16[24,256,256]{2,1,0:T(8,128)(2,1)}, bf16[1,128,1024]{2,1,0:T(8,128)(2,1)}) custom-call(bf16[6,256,256]{2,1,0:T(8,128)(2,1)} %get-tuple-element.152.own, f32[24,256]{1,0:T(8,128)} %left_diag.1, f32[24,256]{1,0:T(8,128)} %right_diag.1, bf16[1,128,1024]{2,1,0:T(8,128)(2,1)} %get-tuple-element.153.grad_in), custom_call_target="tpu_custom_call" | custom-call | flops 32212254720 | bytes 10485760 | tf_op jit(solution)/shard_map/shampoo/pallas_call | solution.py:1897
  466.0 1.8 convert_element_type.28
  467.8 0.6 reshape.49.left_diag
  468.4 0.6 reshape.50.right_diag
  469.1 15.1 %finish_slots.1 = (f32[24,256,256]{2,1,0:T(8,128)}, f32[24,256,256]{2,1,0:T(8,128)}, f32[24,256,256]{2,1,0:T(8,128)}, f32[24,256,256]{2,1,0:T(8,128)}, bf16[24,256,256]{2,1,0:T(8,128)(2,1)}) custom-call(bf16[24,256,256]{2,1,0:T(8,128)(2,1)} %get-tuple-element.155.grad, bf16[24,256,256]{2,1,0:T(8,128)(2,1)} %get-tuple-element.156.move, ...), custom_call_target="tpu_custom_call" | custom-call | flops 2147483648 | bytes 40894464 | tf_op jit(solution)/shard_map/finish_slots/pallas_call | solution.py:1945
  484.2 0.1 multiply_reduce_fusion
  484.3 0.8 multiply_subtract_fusion
  485.1 0.7 copy.33
  485.8 0.7 copy.34
  486.5 0.6 copy.35
  (15 shorter events, 0.0 us)
Async XLA Ops:
  258.5 25.0 %copy-start.5 = (s32[192]{0:T(256)S(1)}, s32[192]{0:T(256)}, u32[]{:S(2)}) copy-start(s32[192]{0:T(256)} %slots.9) | copy-start | bytes 2308
  417.3 50.5 %copy-start.6 = (f32[24,256]{1,0:T(8,128)S(1)}, f32[24,256]{1,0:T(8,128)}, u32[]{:S(2)}) copy-start(f32[24,256]{1,0:T(8,128)} %left_diag.1) | copy-start | bytes 73732
  417.3 51.1 %copy-start.7 = (f32[24,256]{1,0:T(8,128)S(1)}, f32[24,256]{1,0:T(8,128)}, u32[]{:S(2)}) copy-start(f32[24,256]{1,0:T(8,128)} %right_diag.1) | copy-start | bytes 73732
  469.0 15.1 %copy-start.1 = (f32[20,1024]{1,0:T(8,128)S(1)}, f32[20,1024]{1,0:T(8,128)}, u32[]{:S(2)}) copy-start(f32[20,1024]{1,0:T(8,128)} %get-tuple-element.186) | copy-start | bytes 245764
  469.0 15.3 %copy-start = (f32[20,1024]{1,0:T(8,128)S(1)}, f32[20,1024]{1,0:T(8,128)}, u32[]{:S(2)}) copy-start(f32[20,1024]{1,0:T(8,128)} %vecs.9) | copy-start | bytes 245764
  469.0 15.3 %copy-start.4 = (f32[20,1024]{1,0:T(8,128)S(1)}, f32[20,1024]{1,0:T(8,128)}, u32[]{:S(2)}) copy-start(f32[20,1024]{1,0:T(8,128)} %param.21) | copy-start | bytes 245764
  469.0 16.1 %copy-start.2 = (bf16[1,128,1024]{2,1,0:T(8,128)(2,1)S(1)}, bf16[1,128,1024]{2,1,0:T(8,128)(2,1)}, u32[]{:S(2)}) copy-start(bf16[1,128,1024]{2,1,0:T(8,128)(2,1)} %get-tuple-element.178) | copy-start | bytes 786436
  469.1 16.8 %copy-start.3 = (bf16[1,128,1024]{2,1,0:T(8,128)(2,1)S(1)}, bf16[1,128,1024]{2,1,0:T(8,128)(2,1)}, u32[]{:S(2)}) copy-start(bf16[1,128,1024]{2,1,0:T(8,128)(2,1)} %get-tuple-element.179) | copy-start | bytes 786436

commit v2 on v0

--- a/solution.py
+++ b/solution.py
@@ -1,8 +1,12 @@
+import functools
 import math
 
 import jax
+import ml_dtypes
 import jax.numpy as jnp
 from jax import lax
+from jax.experimental import pallas as pl
+from jax.experimental.pallas import tpu as pltpu
 from jax.sharding import PartitionSpec as P
 
 D = 1024
@@ -218,7 +222,376 @@
     return (left_new, right_new, weight - step_rate * ratio * direction)
 
 
-def local(
+MESH = pl.DeviceIdType.MESH
+LOW = jnp.bfloat16
+FULL = jnp.float32
+VMEM_ASK = 60 * 1024 * 1024
+GROUP = 24
+HALF = 12
+QUART = 4
+
+
+def place():
+    samp = lax.axis_index("samp")
+    blk = lax.axis_index("blk")
+    return (lax.div(samp, 2), lax.rem(samp, 2), lax.div(blk, 2), lax.rem(blk, 2))
+
+
+def meet(devices):
+    barrier = pltpu.get_barrier_semaphore()
+    for device in devices:
+        pl.semaphore_signal(barrier, inc=1, device_id=device, device_id_type=MESH)
+    pl.semaphore_wait(barrier, len(devices))
+
+
+def meet_all():
+    barrier = pltpu.get_barrier_semaphore()
+    samp = lax.axis_index("samp")
+    blk = lax.axis_index("blk")
+
+    def tell(at, carry):
+        to = lax.rem(samp * 8 + blk + at, 32)
+        pl.semaphore_signal(
+            barrier, inc=1, device_id=(lax.div(to, 8), lax.rem(to, 8)), device_id_type=MESH
+        )
+        return carry
+
+    lax.fori_loop(1, 32, tell, 0)
+    pl.semaphore_wait(barrier, 31)
+
+
+def turned_pair(n):
+    return 2 * lax.rem(n, 2) + lax.div(n, 2)
+
+
+class Swap:
+    def __init__(self, local_sems, send_sems, recv_sems, first=0):
+        x, c, z, y = place()
+        self.first = first
+        self.stays = z == turned_pair(2 * x + c)
+        self.to = (turned_pair(z), 2 * turned_pair(2 * x + c) + y)
+        self.sems = (local_sems, send_sems, recv_sems)
+        self.pairs = []
+
+    def start(self, src, dst):
+        at = self.first + len(self.pairs)
+        local_sems, send_sems, recv_sems = self.sems
+        local = pltpu.make_async_copy(src, dst, local_sems.at[at])
+        away = pltpu.make_async_remote_copy(
+            src_ref=src, dst_ref=dst, send_sem=send_sems.at[at], recv_sem=recv_sems.at[at],
+            device_id=self.to, device_id_type=MESH,
+        )
+        self.pairs.append((local, away))
+
+        @pl.when(self.stays)
+        def keep():
+            local.start()
+
+        @pl.when(jnp.logical_not(self.stays))
+        def send():
+            away.start()
+
+    def finish(self):
+        @pl.when(self.stays)
+        def kept():
+            for local, away in self.pairs:
+                local.wait()
+
+        @pl.when(jnp.logical_not(self.stays))
+        def sent():
+            for local, away in self.pairs:
+                away.wait()
+
+
+def push(src, dst, send, recv, device):
+    copy = pltpu.make_async_remote_copy(
+        src_ref=src, dst_ref=dst, send_sem=send, recv_sem=recv, device_id=device, device_id_type=MESH
+    )
+    copy.start()
+    return copy
+
+
+FIRST, SECOND, BOTH, CROSS = range(4)
+SIZES = (2, 2, 3, 1)
+
+
+def gather_blocks(r, notes, while_last):
+    x, c, z, y = place()
+    samp = 2 * x + c
+    blk = 2 * z + y
+    to_y = (samp, 2 * z + 1 - y)
+    to_x = (2 * (1 - x) + c, blk)
+    to_c = (2 * x + 1 - c, blk)
+    base = c * HALF
+    out = r.weights
+    starts = (base + x * 8, base + x * 8 + 2, base + QUART, base + QUART + 3)
+    far_starts = (base + (1 - x) * 8, base + (1 - x) * 8 + 2)
+    other = (1 - c) * HALF
+    parts = [base + x * 8, base + QUART, base + (1 - x) * 8, other, other + QUART, other + 2 * QUART]
+    notes_out, note_send, note_recv = r.notes_land, r.note_send, r.note_recv
+
+    def load(at):
+        return pltpu.make_async_copy(
+            r.masters.at[pl.ds(parts[at], QUART)], r.wide.at[at % 2], r.load_sems.at[at]
+        )
+
+    def ready(at):
+        load(at).wait()
+        out[pl.ds(blk * GROUP + parts[at], QUART)] = r.wide[at % 2].astype(LOW)
+        if at + 2 < len(parts):
+            load(at + 2).start()
+
+    def copy(group, start, size, sems, at, device):
+        place_out = out.at[pl.ds(group * GROUP + start, size)]
+        return pltpu.make_async_remote_copy(
+            src_ref=place_out, dst_ref=place_out,
+            send_sem=sems.at[(0,) + at], recv_sem=sems.at[(1,) + at], device_id=device, device_id_type=MESH,
+        )
+
+    def z_copy(kind, way, origin):
+        to = (samp, blk + (2 if way == 0 else -2))
+        return copy(2 * origin + y, starts[kind], SIZES[kind], r.z_sems, (kind, way, origin), to)
+
+    def z_cross(way, origin, side):
+        to = (samp, blk + (2 if way == 0 else -2))
+        return copy(2 * origin + side, starts[CROSS], 1, r.z_sems, (CROSS + side, way, origin), to)
+
+    def y_copy(kind, origin):
+        return copy(2 * origin + y, starts[kind], SIZES[kind], r.y_sems, (kind, origin), to_y)
+
+    def y_landed(kind, origin):
+        return copy(2 * origin + 1 - y, starts[kind], SIZES[kind], r.y_sems, (kind, origin), to_y)
+
+    def x_copy(kind, group):
+        return copy(group, starts[kind], SIZES[kind], r.x_sems, (kind, group), to_x)
+
+    def x_landed(kind, group):
+        return copy(group, far_starts[kind], SIZES[kind], r.x_sems, (kind, group), to_x)
+
+    def core_copy(kind, group):
+        return copy(group, starts[kind], SIZES[kind], r.core_sems, (kind, group), to_c)
+
+    def far_copy(kind, group):
+        return copy(group, far_starts[kind], SIZES[kind], r.far_sems, (kind, group), to_c)
+
+    def on_from_here(kind, group):
+        if kind in (FIRST, SECOND):
+            x_copy(kind, group).start()
+        core_copy(kind, group).start()
+
+    def begin(kind):
+        @pl.when(z < 3)
+        def up():
+            z_copy(kind, 0, z).start()
+
+        @pl.when(z > 0)
+        def down():
+            z_copy(kind, 1, z).start()
+
+        y_copy(kind, z).start()
+
+    def z_step(kind, distance):
+        for way in (0, 1):
+            origin = z - distance if way == 0 else z + distance
+
+            @pl.when(origin >= 0 if way == 0 else origin <= 3)
+            def arrived():
+                z_copy(kind, way, origin).wait_recv()
+
+                @pl.when(z < 3 if way == 0 else z > 0)
+                def onward():
+                    z_copy(kind, way, origin).start()
+
+                y_copy(kind, origin).start()
+                on_from_here(kind, 2 * origin + y)
+
+    def y_step(kind, distance):
+        for way in (0, 1):
+            origin = z - distance if way == 0 else z + distance
+
+            @pl.when(origin >= 0 if way == 0 else origin <= 3)
+            def arrived():
+                y_landed(kind, origin).wait_recv()
+                on_from_here(kind, 2 * origin + 1 - y)
+
+    def y_own(kind):
+        y_landed(kind, z).wait_recv()
+        on_from_here(kind, 2 * z + 1 - y)
+
+    def cross_step(distance):
+        for side in (0, 1):
+            for way in (0, 1):
+                origin = z - distance if way == 0 else z + distance
+
+                @pl.when(origin >= 0 if way == 0 else origin <= 3)
+                def arrived():
+                    z_cross(way, origin, side).wait_recv()
+
+                    @pl.when(z < 3 if way == 0 else z > 0)
+                    def onward():
+                        z_cross(way, origin, side).start()
+
+                    core_copy(CROSS, 2 * origin + side).start()
+
+    def x_step(kind, distance, same):
+        for way in (0, 1):
+            origin = z - distance if way == 0 else z + distance
+
+            @pl.when(origin >= 0 if way == 0 else origin <= 3)
+            def arrived():
+                group = 2 * origin + (y if same else 1 - y)
+                x_landed(kind, group).wait_recv()
+                far_copy(kind, group).start()
+
+    def x_own(kind):
+        x_landed(kind, 2 * z + 1 - y).wait_recv()
+        far_copy(kind, 2 * z + 1 - y).start()
+
+    note_local = pltpu.make_async_copy(notes, notes_out.at[blk], r.load_sems.at[6])
+
+    def note_copy(j, origin):
+        return pltpu.make_async_remote_copy(
+            src_ref=notes, dst_ref=notes_out.at[origin], send_sem=note_send.at[j], recv_sem=note_recv.at[origin],
+            device_id=(j // 2, 2 * turned_pair(samp) + j % 2), device_id_type=MESH,
+        )
+
+    stays = z == turned_pair(samp)
+
+    def is_me(j):
+        return jnp.logical_and(stays, 2 * samp + y == j)
+
+    def here_from(j):
+        return jnp.logical_and(stays, blk == j)
+
+    load(0).start()
+    load(1).start()
+    meet_all()
+    r.swap_rows.start(r.rows_in, r.rows_land)
+    ready(0)
+    begin(FIRST)
+    begin(SECOND)
+    ready(1)
+    y_copy(CROSS, z).start()
+    for j in range(8):
+
+        @pl.when(jnp.logical_not(is_me(j)))
+        def send_note():
+            note_copy(j, blk).start()
+
+    @pl.when(stays)
+    def keep_note():
+        note_local.start()
+
+    for at in range(2, len(parts)):
+        ready(at)
+    z_step(FIRST, 1)
+    y_own(FIRST)
+    z_step(SECOND, 1)
+    y_own(SECOND)
+    begin(BOTH)
+    y_landed(CROSS, z).wait_recv()
+    core_copy(CROSS, 2 * z + 1 - y).start()
+    for way, there in ((0, z < 3), (1, z > 0)):
+        for side in (0, 1):
+            @pl.when(there)
+            def both_sides():
+                z_cross(way, z, side).start()
+
+    z_step(FIRST, 2)
+    y_step(FIRST, 1)
+    z_step(SECOND, 2)
+    y_step(SECOND, 1)
+    x_own(FIRST)
+    z_step(FIRST, 3)
+    x_own(SECOND)
+    y_step(FIRST, 2)
+    z_step(SECOND, 3)
+    x_step(FIRST, 1, True)
+    y_step(SECOND, 2)
+    x_step(SECOND, 1, True)
+    y_step(FIRST, 3)
+    y_step(SECOND, 3)
+    z_step(BOTH, 1)
+    x_step(FIRST, 1, False)
+    x_step(FIRST, 2, True)
+    y_own(BOTH)
+    cross_step(1)
+    x_step(SECOND, 1, False)
+    x_step(SECOND, 2, True)
+    z_step(BOTH, 2)
+    x_step(FIRST, 3, True)
+    y_step(BOTH, 1)
+    cross_step(2)
+    x_step(FIRST, 2, False)
+    z_step(BOTH, 3)
+    x_step(SECOND, 3, True)
+    y_step(BOTH, 2)
+    x_step(SECOND, 2, False)
+    cross_step(3)
+    x_step(FIRST, 3, False)
+    y_step(BOTH, 3)
+    x_step(SECOND, 3, False)
+
+    while_last()
+    other_starts = (other + x * 8, other + x * 8 + 2, other + QUART, other + QUART + 3)
+    other_far = (other + (1 - x) * 8, other + (1 - x) * 8 + 2)
+
+    def settle(group, carry):
+        @pl.when(group != blk)
+        def other_group():
+            for kind in range(4):
+                copy(group, other_starts[kind], SIZES[kind], r.core_sems, (kind, group), to_c).wait_recv()
+                core_copy(kind, group).wait_send()
+            for kind in (FIRST, SECOND):
+                copy(group, other_far[kind], SIZES[kind], r.far_sems, (kind, group), to_c).wait_recv()
+                far_copy(kind, group).wait_send()
+                x_copy(kind, group).wait_send()
+
+        return carry
+
+    lax.fori_loop(0, 8, settle, 0)
+
+    def sent_along(origin, carry):
+        for kind in (FIRST, SECOND, BOTH):
+            y_copy(kind, origin).wait_send()
+
+            @pl.when(jnp.logical_and(origin <= z, z < 3))
+            def up():
+                z_copy(kind, 0, origin).wait_send()
+
+            @pl.when(jnp.logical_and(origin >= z, z > 0))
+            def down():
+                z_copy(kind, 1, origin).wait_send()
+
+        for side in (0, 1):
+            @pl.when(jnp.logical_and(origin <= z, z < 3))
+            def cross_up():
+                z_cross(0, origin, side).wait_send()
+
+            @pl.when(jnp.logical_and(origin >= z, z > 0))
+            def cross_down():
+                z_cross(1, origin, side).wait_send()
+
+        return carry
+
+    lax.fori_loop(0, 4, sent_along, 0)
+    y_copy(CROSS, z).wait_send()
+    for j in range(8):
+
+        @pl.when(jnp.logical_not(is_me(j)))
+        def sent_note():
+            note_copy(j, blk).wait_send()
+
+        @pl.when(jnp.logical_not(here_from(j)))
+        def got_note():
+            note_copy(j, j).wait_recv()
+
+    @pl.when(stays)
+    def kept_note():
+        note_local.wait()
+
+
+def local_any(
     inputs,
     cot_first,
     cot_second,
@@ -466,6 +839,1040 @@
     )
 
 
+TOKENS = 128
+PAIR = 2 * HD
+SEQ_ALL = 8 * TOKENS
+QKV_AT, OUT_AT, UP_AT, DOWN_AT = 0, 48, 64, 128
+WIDE = D // BS
+DEEP = FF // BS
+LEAD_AT = 8 + FF // D
+
+
+def dot(left, right):
+    return jnp.dot(left, right, preferred_element_type=FULL)
+
+
+def dot_t(left, right):
+    return lax.dot_general(left, right, (((1,), (1,)), ((), ())), preferred_element_type=FULL)
+
+
+def normal(value):
+    centred = value - jnp.mean(value, axis=-1, keepdims=True)
+    rate = lax.rsqrt(jnp.mean(centred * centred, axis=-1, keepdims=True) + 1e-06)
+    return (centred * rate, rate)
+
+
+def normal_back(grad, unit, rate, gain):
+    scaled = grad * gain
+    return rate * (
+        scaled
+        - jnp.mean(scaled, axis=-1, keepdims=True)
+        - unit * jnp.mean(scaled * unit, axis=-1, keepdims=True)
+    )
+
+
+def total(value):
+    return jnp.sum(value, axis=0, keepdims=True)
+
+
+def gelu_parts(value):
+    phi = 0.5 + 0.5 * lax.erf(value * (0.5**0.5))
+    return phi, value * phi
+
+
+def gelu_slope(value):
+    phi, unused = gelu_parts(value)
+    return phi + value * jnp.exp(-0.5 * value * value) * ((2.0 * math.pi) ** -0.5)
+
+
+class Weights:
+    def __init__(self, slots, held):
+        self.slots, self.held = slots, held
+
+    def block(self, base, cols, row, col):
+        return self.held[self.slots[base + row * cols + col]]
+
+    def down_col(self, base, rows, cols, col):
+        return jnp.concatenate([self.block(base, cols, row, col) for row in range(rows)], axis=0)
+
+    def along_row(self, base, cols, row, first=0, last=None):
+        return jnp.concatenate(
+            [self.block(base, cols, row, col) for col in range(first, cols if last is None else last)], axis=1
+        )
+
+
+def lead_row(vecs, lead):
+    row = jnp.zeros((1, D), FULL)
+    for at in range(LEADS):
+        row = row + jnp.where(lead == at, vecs[LEAD_AT + at : LEAD_AT + at + 1], 0.0)
+    return row
+
+
+def project(r, layer, hidden, vecs, weights):
+    unit, unused = normal(hidden)
+    normed = unit * vecs[0:1] + vecs[1:2]
+    for k in range(WIDE):
+        r.left_held[layer, k] = normed[:, k * BS : (k + 1) * BS].T.astype(LOW)
+    give_pool(r, True, layer, 0)
+    normed = normed.astype(LOW)
+    for step in range(WIDE):
+        within = lax.rem(step + lax.div(r.plane.me, 2), WIDE)
+        cols = pl.ds(pl.multiple_of(within * BS, BS), BS)
+        for kind in range(3):
+            part = dot(normed, weights.down_col(QKV_AT, WIDE, 3 * WIDE, kind * WIDE + within))
+            if kind != 1:
+                row = 2 if kind == 0 else 3
+                part = part + vecs[row : row + 1, cols]
+            part = part.astype(LOW)
+            for half in range(2):
+                r.packed[2 * within + half, :, kind * PAIR : (kind + 1) * PAIR] = part[
+                    :, half * PAIR : (half + 1) * PAIR
+                ]
+        for half in range(2):
+            r.plane.send_or_keep(r.packed, r.held[layer], r.in_sems[layer], 2 * within + half)
+
+
+def pool_at(left, kind):
+    counts, bases = (LEFTS, LEFT_AT) if left else (RIGHTS, RIGHT_AT)
+    return pl.ds(bases[kind], counts[kind])
+
+
+def pool_copies(r, left, layer, kind):
+    x, c, z, y = place()
+    ids = pool_at(left, kind)
+    at = (0 if left else 8) + 4 * layer + kind
+    source = (r.left_held if left else r.right_held).at[layer, ids]
+
+    def target(part):
+        tokens = pl.ds((2 * part + layer) * TOKENS, TOKENS)
+        return r.left_pool.at[ids, :, tokens] if left else r.right_pool.at[ids, tokens]
+
+    here = pltpu.make_async_copy(source, target(0), r.pool_sems.at[0, at])
+    there = pltpu.make_async_remote_copy(
+        src_ref=source, dst_ref=target(1), send_sem=r.pool_sems.at[1, at], recv_sem=r.pool_sems.at[2, at],
+        device_id=(2 * x + 1 - c, 2 * z + y), device_id_type=MESH,
+    )
+    return here, there
+
+
+def give_pool(r, left, layer, kind):
+    for copy in pool_copies(r, left, layer, kind):
+        copy.start()
+
+
+def feed(r, layer, hidden, vecs, weights, u_held):
+    attended = jnp.concatenate([r.o_land[j] for j in range(8)], axis=1)
+    for k in range(WIDE):
+        r.left_held[layer, WIDE + k] = attended[:, k * BS : (k + 1) * BS].astype(FULL).T.astype(LOW)
+    give_pool(r, True, layer, 1)
+    branch = [dot(attended, weights.down_col(OUT_AT, WIDE, WIDE, n)) for n in range(WIDE)]
+    middle = hidden + jnp.concatenate(branch, axis=1) + vecs[4:5]
+    unit, unused = normal(middle)
+    normed = unit * vecs[5:6] + vecs[6:7]
+    for k in range(WIDE):
+        r.left_held[layer, 2 * WIDE + k] = normed[:, k * BS : (k + 1) * BS].T.astype(LOW)
+    give_pool(r, True, layer, 2)
+    normed = normed.astype(LOW)
+    per = D // BS
+    for f in range(DEEP):
+        bias = vecs[8 + f // per : 9 + f // per, (f % per) * BS : (f % per + 1) * BS]
+        upward = dot(normed, weights.down_col(UP_AT, WIDE, DEEP, f)) + bias
+        u_held[f] = upward
+        activated = gelu_parts(upward)[1]
+        r.act_held[:, f * BS : (f + 1) * BS] = activated.astype(LOW)
+        r.left_held[layer, 3 * WIDE + f] = activated.T.astype(LOW)
+    give_pool(r, True, layer, 3)
+    branch = [dot(r.act_held[...], weights.down_col(DOWN_AT, DEEP, WIDE, n)) for n in range(WIDE)]
+    return middle, middle + jnp.concatenate(branch, axis=1) + vecs[7:8]
+
+
+def feed_back(r, layer, grad_out, middle, u_in, vecs, weights):
+    rows = r.rows
+    grad_two = grad_out.astype(LOW)
+    for k in range(WIDE):
+        r.right_held[layer, RIGHT_AT[3] + k] = grad_two[:, k * BS : (k + 1) * BS]
+    give_pool(r, False, layer, 3)
+    rows[7:8] += total(grad_two.astype(FULL))
+    per = D // BS
+    for f in range(DEEP):
+        grad_act = dot_t(grad_two, weights.along_row(DOWN_AT, WIDE, f))
+        grad_up = (grad_act * gelu_slope(u_in[f])).astype(LOW)
+        r.right_held[layer, RIGHT_AT[2] + f] = grad_up
+        rows[8 + f // per : 9 + f // per, (f % per) * BS : (f % per + 1) * BS] += total(grad_up.astype(FULL))
+    give_pool(r, False, layer, 2)
+    grad_up = jnp.concatenate([r.right_held[layer, RIGHT_AT[2] + f] for f in range(DEEP)], axis=1)
+    grad_normed = jnp.concatenate(
+        [dot_t(grad_up, weights.along_row(UP_AT, DEEP, k)) for k in range(WIDE)], axis=1
+    )
+    unit, rate = normal(middle)
+    rows[5:6] += total(grad_normed * unit)
+    rows[6:7] += total(grad_normed)
+    grad_middle = grad_out + normal_back(grad_normed, unit, rate, vecs[5:6])
+    grad_one = grad_middle.astype(LOW)
+    for k in range(WIDE):
+        r.right_held[layer, RIGHT_AT[1] + k] = grad_one[:, k * BS : (k + 1) * BS]
+    give_pool(r, False, layer, 1)
+    rows[4:5] += total(grad_one.astype(FULL))
+    for k in range(WIDE):
+        part = dot_t(grad_one, weights.along_row(OUT_AT, WIDE, k)).astype(LOW)
+        for half in range(2):
+            r.do_message[2 * k + half] = part[:, half * PAIR : (half + 1) * PAIR]
+            r.plane.send_or_keep(r.do_message, r.do_land, r.do_sems[layer], 2 * k + half)
+    return grad_middle
+
+
+def project_back(r, layer, grad_middle, hidden, vecs, weights, lead):
+    rows = r.rows
+
+    def blocks_of_kind(kind):
+        source, cols = (r.dq_land, slice(0, PAIR)) if kind == 0 else (r.dkv_land, slice((kind - 1) * PAIR, kind * PAIR))
+        for within in range(WIDE):
+            part = jnp.concatenate([source[2 * within, :, cols], source[2 * within + 1, :, cols]], axis=1)
+            r.right_held[layer, kind * WIDE + within] = part
+            if kind != 1:
+                row = 2 if kind == 0 else 3
+                rows[row : row + 1, within * BS : (within + 1) * BS] += total(part.astype(FULL))
+
+    def back(first, last):
+        part = jnp.concatenate([r.right_held[layer, n] for n in range(first, last)], axis=1)
+        return jnp.concatenate(
+            [dot_t(part, weights.along_row(QKV_AT, 3 * WIDE, k, first, last)) for k in range(WIDE)], axis=1
+        )
+
+    r.plane.received(r.dkv_land, r.dkv_sems[layer])
+    blocks_of_kind(1)
+    blocks_of_kind(2)
+    grad_normed = back(WIDE, 3 * WIDE)
+    r.plane.received(r.dq_land, r.dq_sems[layer])
+    blocks_of_kind(0)
+    give_pool(r, False, layer, 0)
+    grad_normed = grad_normed + back(0, WIDE)
+    unit, rate = normal(hidden)
+    rows[0:1] += total(grad_normed * unit)
+    rows[1:2] += total(grad_normed)
+    grad_hidden = grad_middle + normal_back(grad_normed, unit, rate, vecs[0:1])
+    sums = total(grad_hidden)
+    for at in range(LEADS):
+        rows[LEAD_AT + at : LEAD_AT + at + 1] += jnp.where(lead == at, sums, 0.0)
+    return grad_hidden
+
+
+def attend(r, layer):
+    held, turned, stats = r.held[layer], r.turned[layer], r.stats[layer]
+    plane = r.plane
+    plane.received(held, r.in_sems[layer])
+    both = held[...].reshape(SEQ_ALL, 3 * PAIR)
+    queries = both[:, :PAIR].astype(FULL)
+    keys = both[:, PAIR : 2 * PAIR].astype(FULL)
+    values_t = both[:, 2 * PAIR :].astype(FULL).T.astype(LOW)
+    for head in range(2):
+        q_side, k_side, unused = head_sides(queries, keys, r.neg[...], head)
+        r.query_side[head] = q_side.astype(LOW)
+        r.key_side[head] = k_side.astype(LOW)
+
+    def chunk(step, carry):
+        at = lax.rem(step + lax.div(plane.me, 2), 4)
+        first = pl.multiple_of(at * BS, BS)
+        for head in range(2):
+            scores = dot_t(r.key_side[head], r.query_side[head, pl.ds(first, BS)])
+            most = jnp.max(scores, axis=0, keepdims=True)
+            expos = jnp.exp(scores - most)
+            sums = jnp.sum(expos, axis=0, keepdims=True)
+            part = dot(values_t[head * HD : (head + 1) * HD], expos.astype(LOW)) / sums
+            turned[at, head * HD : (head + 1) * HD] = part
+            stats[head : head + 1, pl.ds(first, BS)] = most + jnp.log(sums)
+        for half in range(2):
+            to = 2 * at + half
+            r.o_message[to] = turned[at, :, half * TOKENS : (half + 1) * TOKENS].T.astype(LOW)
+            plane.send_or_keep(r.o_message, r.o_land, r.o_sems[layer], to)
+        return carry
+
+    lax.fori_loop(0, SEQ_ALL // BS, chunk, 0)
+    plane.sent(r.packed, r.in_sems[layer])
+    plane.received(r.o_land, r.o_sems[layer])
+    plane.sent(r.o_message, r.o_sems[layer])
+
+
+def attend_back(r, layer):
+    held, turned, stats = r.held[layer], r.turned[layer], r.stats[layer]
+    plane = r.plane
+    both = held[...].reshape(SEQ_ALL, 3 * PAIR)
+    queries = both[:, :PAIR].astype(FULL)
+    keys = both[:, PAIR : 2 * PAIR].astype(FULL)
+    keys_t = keys.T.astype(LOW)
+    r.grad_q[...] = jnp.zeros_like(r.grad_q)
+    for head in range(2):
+        q_side, k_side, own = head_sides(queries, keys, r.neg[...], head)
+        r.query_side[head] = q_side.astype(LOW)
+        r.query_plain[head] = jnp.where(own, q_side, 0.0).astype(LOW)
+        r.key_side[head] = k_side.astype(LOW)
+    plane.received(r.do_land, r.do_sems[layer])
+    grads = r.do_land[...].reshape(SEQ_ALL, PAIR).astype(FULL)
+    lane = lax.broadcasted_iota(jnp.int32, grads.shape, 1)
+    r.do_side[0] = jnp.where(lane < HD, grads, 0.0).astype(LOW)
+    r.do_side[1] = jnp.where(lane >= HD, grads, 0.0).astype(LOW)
+    grads_t = grads.T
+    inner = []
+    for head in range(2):
+        side = slice(head * HD, (head + 1) * HD)
+        inner.append(
+            jnp.concatenate(
+                [
+                    jnp.sum(turned[at, side] * grads_t[side, at * BS : (at + 1) * BS], axis=0, keepdims=True)
+                    for at in range(SEQ_ALL // BS)
+                ],
+                axis=1,
+            )
+        )
+    left = lax.broadcasted_iota(jnp.int32, (BS, PAIR), 1) < HD
+    keys_held = [keys_t[head * HD : (head + 1) * HD] for head in range(2)]
+    for at in range(SEQ_ALL // BS):
+        first = at * BS
+        grad_k = []
+        grad_v = None
+        values = held[2 * at : 2 * at + 2, :, 2 * PAIR :].reshape(BS, PAIR)
+        for head in range(2):
+            scores = dot_t(r.key_side[head, first : first + BS], r.query_side[head])
+            probs = jnp.exp(scores - stats[head : head + 1])
+            dprobs = dot_t(values, r.do_side[head])
+            dscores = (probs * (dprobs - inner[head])).astype(LOW)
+            term = dot(probs.astype(LOW), r.do_side[head])
+            grad_v = term if grad_v is None else grad_v + term
+            grad_k.append(dot(dscores, r.query_plain[head]))
+            r.grad_q[head * HD : (head + 1) * HD] += dot(keys_held[head][:, first : first + BS], dscores)
+        grad_k = jnp.where(left, grad_k[0], grad_k[1]).astype(LOW)
+        grad_v = grad_v.astype(LOW)
+        for half in range(2):
+            to = 2 * at + half
+            rows = slice(half * TOKENS, (half + 1) * TOKENS)
+            r.dkv_message[to, :, :PAIR] = grad_k[rows]
+            r.dkv_message[to, :, PAIR:] = grad_v[rows]
+            plane.send_or_keep(r.dkv_message, r.dkv_land, r.dkv_sems[layer], to)
+    for j in range(8):
+        r.dq_message[j] = (r.grad_q[:, j * TOKENS : (j + 1) * TOKENS].T * HD**-0.5).astype(LOW)
+        plane.send_or_keep(r.dq_message, r.dq_land, r.dq_sems[layer], j)
+
+
+class Refs:
+    pass
+
+
+SCRATCH = (
+    ("weights", pltpu.VMEM((NB, BS, BS), LOW)),
+    ("wide", pltpu.VMEM((2, QUART, BS, BS), FULL)),
+    ("notes_land", pltpu.VMEM((8, 8, TOKENS), FULL)),
+    ("rows_land", pltpu.VMEM((1, TOKENS, D), LOW)),
+    ("first_land", pltpu.VMEM((1, TOKENS, D), LOW)),
+    ("second_land", pltpu.VMEM((1, TOKENS, D), LOW)),
+    ("pred_one", pltpu.VMEM((1, TOKENS, D), LOW)),
+    ("pred_two", pltpu.VMEM((1, TOKENS, D), LOW)),
+    ("hidden_one", pltpu.VMEM((TOKENS, D), FULL)),
+    ("hidden_two", pltpu.VMEM((TOKENS, D), FULL)),
+    ("middle_one", pltpu.VMEM((TOKENS, D), FULL)),
+    ("u_one", pltpu.VMEM((DEEP, TOKENS, BS), FULL)),
+    ("u_two", pltpu.VMEM((DEEP, TOKENS, BS), FULL)),
+    ("act_held", pltpu.VMEM((TOKENS, FF), LOW)),
+    ("left_held", pltpu.VMEM((2, 3 * WIDE + DEEP, BS, TOKENS), LOW)),
+    ("right_held", pltpu.VMEM((2, 5 * WIDE + DEEP, TOKENS, BS), LOW)),
+    ("packed", pltpu.VMEM((8, TOKENS, 3 * PAIR), LOW)),
+    ("held", pltpu.VMEM((2, 8, TOKENS, 3 * PAIR), LOW)),
+    ("turned", pltpu.VMEM((2, SEQ_ALL // BS, PAIR, BS), FULL)),
+    ("stats", pltpu.VMEM((2, 8, SEQ_ALL), FULL)),
+    ("o_message", pltpu.VMEM((8, TOKENS, PAIR), LOW)),
+    ("o_land", pltpu.VMEM((8, TOKENS, PAIR), LOW)),
+    ("do_message", pltpu.VMEM((8, TOKENS, PAIR), LOW)),
+    ("do_land", pltpu.VMEM((8, TOKENS, PAIR), LOW)),
+    ("dq_message", pltpu.VMEM((8, TOKENS, PAIR), LOW)),
+    ("dq_land", pltpu.VMEM((8, TOKENS, PAIR), LOW)),
+    ("dkv_message", pltpu.VMEM((8, TOKENS, 2 * PAIR), LOW)),
+    ("dkv_land", pltpu.VMEM((8, TOKENS, 2 * PAIR), LOW)),
+    ("neg", pltpu.VMEM((SEQ_ALL, PAIR), FULL)),
+    ("query_side", pltpu.VMEM((2, SEQ_ALL, PAIR), LOW)),
+    ("query_plain", pltpu.VMEM((2, SEQ_ALL, PAIR), LOW)),
+    ("key_side", pltpu.VMEM((2, SEQ_ALL, PAIR), LOW)),
+    ("do_side", pltpu.VMEM((2, SEQ_ALL, PAIR), LOW)),
+    ("grad_q", pltpu.VMEM((PAIR, SEQ_ALL), FULL)),
+    ("load_sems", pltpu.SemaphoreType.DMA((7,))),
+    ("z_sems", pltpu.SemaphoreType.DMA((2, 5, 2, 4))),
+    ("y_sems", pltpu.SemaphoreType.DMA((2, 4, 4))),
+    ("x_sems", pltpu.SemaphoreType.DMA((2, 2, 8))),
+    ("core_sems", pltpu.SemaphoreType.DMA((2, 4, 8))),
+    ("far_sems", pltpu.SemaphoreType.DMA((2, 2, 8))),
+    ("note_send", pltpu.SemaphoreType.DMA((8,))),
+    ("note_recv", pltpu.SemaphoreType.DMA((8,))),
+    ("swap_local", pltpu.SemaphoreType.DMA((5,))),
+    ("swap_send", pltpu.SemaphoreType.DMA((5,))),
+    ("swap_recv", pltpu.SemaphoreType.DMA((5,))),
+    ("plane_sems", pltpu.SemaphoreType.DMA((5, 2, 2, 8))),
+    ("pool_sems", pltpu.SemaphoreType.DMA((3, 16))),
+)
+INPUTS = ("slots", "masters", "notes", "rows_in", "first_in", "second_in", "vectors")
+OUTPUTS = ("left_pool", "right_pool", "pred_one_out", "pred_two_out", "input_grad", "rows")
+
+
+def model_kernel(*refs):
+    r = Refs()
+    for name, ref in zip(INPUTS + OUTPUTS + tuple(name for name, unused in SCRATCH), refs):
+        setattr(r, name, ref)
+    for name in ("held", "turned", "stats"):
+        setattr(r, name, [getattr(r, name).at[layer] for layer in range(2)])
+    for at, name in enumerate(("in_sems", "o_sems", "do_sems", "dq_sems", "dkv_sems")):
+        setattr(r, name, [r.plane_sems.at[at, layer] for layer in range(2)])
+    swaps = [Swap(r.swap_local, r.swap_send, r.swap_recv, at) for at in range(5)]
+    r.swap_rows = swaps[0]
+    r.plane = Plane()
+    vecs = r.vectors
+    weights = Weights(r.slots, r.weights)
+
+    def while_last():
+        swaps[1].start(r.second_in, r.second_land)
+        swaps[2].start(r.first_in, r.first_land)
+        swaps[0].finish()
+        r.rows[...] = jnp.zeros_like(r.rows)
+        for layer in range(2):
+            r.stats[layer][...] = jnp.zeros((8, SEQ_ALL), FULL)
+
+    gather_blocks(r, r.notes, while_last)
+    mask_columns(r.notes_land, r.neg)
+    leads = [r.notes_land[0, 1:2, at : at + 1] for at in range(2)]
+    r.hidden_one[...] = r.rows_land[0].astype(FULL) + lead_row(vecs, leads[0])
+    project(r, 0, r.hidden_one[...], vecs, weights)
+    attend(r, 0)
+    middle, result = feed(r, 0, r.hidden_one[...], vecs, weights, r.u_one)
+    r.middle_one[...] = middle
+    r.pred_one[0] = result.astype(LOW)
+    swaps[3].start(r.pred_one, r.pred_one_out)
+    r.hidden_two[...] = result + lead_row(vecs, leads[1])
+    project(r, 1, r.hidden_two[...], vecs, weights)
+    attend(r, 1)
+    middle, result = feed(r, 1, r.hidden_two[...], vecs, weights, r.u_two)
+    r.pred_two[0] = result.astype(LOW)
+    swaps[4].start(r.pred_two, r.pred_two_out)
+    swaps[1].finish()
+    grad_middle = feed_back(r, 1, r.second_land[0].astype(FULL), middle, r.u_two, vecs, weights)
+    attend_back(r, 1)
+    grad = project_back(r, 1, grad_middle, r.hidden_two[...], vecs, weights, leads[1])
+    for source, sems in ((r.do_message, r.do_sems), (r.dkv_message, r.dkv_sems), (r.dq_message, r.dq_sems)):
+        r.plane.sent(source, sems[1])
+    swaps[2].finish()
+    grad = grad + r.first_land[0].astype(FULL)
+    grad_middle = feed_back(r, 0, grad, r.middle_one[...], r.u_one, vecs, weights)
+    attend_back(r, 0)
+    grad = project_back(r, 0, grad_middle, r.hidden_one[...], vecs, weights, leads[0])
+    r.input_grad[0] = grad.astype(LOW)
+    for source, sems in ((r.do_message, r.do_sems), (r.dkv_message, r.dkv_sems), (r.dq_message, r.dq_sems)):
+        r.plane.sent(source, sems[0])
+    for left in (True, False):
+        for layer in range(2):
+            for kind in range(4):
+                for copy in pool_copies(r, left, layer, kind):
+                    copy.wait()
+    swaps[3].finish()
+    swaps[4].finish()
+
+
+def model(slots, masters, notes, rows, first, second, vectors):
+    return pl.pallas_call(
+        model_kernel,
+        out_shape=(
+            shape((N_LEFT, BS, 4 * TOKENS)),
+            shape((N_RIGHT, 4 * TOKENS, BS)),
+            SHAPES["pred"],
+            SHAPES["pred"],
+            SHAPES["pred"],
+            SHAPES["rows"],
+        ),
+        in_specs=[SMEM_IN] + [ANY_AT] * 5 + [VMEM_AT],
+        out_specs=(ANY_AT,) * 4 + (VMEM_AT,) * 2,
+        scratch_shapes=[spec for unused, spec in SCRATCH],
+        compiler_params=pltpu.CompilerParams(
+            collective_id=0, has_side_effects=True, vmem_limit_bytes=63 * 1024 * 1024
+        ),
+        cost_estimate=pl.CostEstimate(flops=24 << 30, bytes_accessed=60 << 20, transcendentals=1 << 23),
+        name="model",
+    )(slots, masters, notes, rows, first, second, vectors)
+
+
+SMEM_IN = pl.BlockSpec(memory_space=pltpu.SMEM)
+VMEM_AT = pl.BlockSpec(memory_space=pltpu.VMEM)
+ANY_AT = pl.BlockSpec(memory_space=pl.ANY)
+
+
+def shape(dims, kind=LOW):
+    return jax.ShapeDtypeStruct(dims, kind)
+
+
+SHAPES = {"pred": shape((1, TOKENS, D)), "rows": shape((20, D), FULL)}
+
+
+def bias_pieces():
+    left = masked
+    pieces = []
+    for unused in range(3):
+        piece = float(ml_dtypes.bfloat16(left))
+        pieces.append(piece)
+        left -= piece
+    assert left == 0.0
+    return pieces
+
+
+MASK_PIECES = bias_pieces()
+
+
+def head_sides(queries, keys, neg, head):
+    lane = lax.broadcasted_iota(jnp.int32, queries.shape, 1)
+    own = (lane < HD) if head == 0 else (lane >= HD)
+    spot = lane - (HD if head == 0 else 0)
+    key_side = jnp.zeros_like(keys)
+    for at, piece in enumerate(MASK_PIECES):
+        key_side = jnp.where(spot == at, neg * piece, key_side)
+    key_side = jnp.where(own, keys, key_side)
+    ones = jnp.where((spot >= 0) & (spot < 3), 1.0, 0.0)
+    query_side = jnp.where(own, queries * HD**-0.5, ones)
+    return query_side, key_side, own
+
+
+class Plane:
+    def __init__(self):
+        x, c, z, y = place()
+        self.z = z
+        self.me = 4 * c + 2 * x + y
+
+    def device(self, j):
+        return (turned_pair(lax.div(j, 2)), 2 * self.z + lax.rem(j, 2))
+
+    def other(self, step):
+        return lax.rem(self.me + step, 8)
+
+    def others(self):
+        return [self.device(self.other(step)) for step in range(1, 8)]
+
+    def copy(self, src, dst, sems, send_at, recv_at, to):
+        return pltpu.make_async_remote_copy(
+            src_ref=src, dst_ref=dst, send_sem=sems.at[0, send_at], recv_sem=sems.at[1, recv_at],
+            device_id=self.device(to), device_id_type=MESH,
+        )
+
+    def send(self, source, target, sems, to):
+        self.copy(source.at[to], target.at[self.me], sems, to, self.me, to).start()
+
+    def send_or_keep(self, source, target, sems, to):
+        @pl.when(to != self.me)
+        def away():
+            self.send(source, target, sems, to)
+
+        @pl.when(to == self.me)
+        def keep():
+            target[to] = source[to]
+
+    def received(self, target, sems):
+        for step in range(1, 8):
+            j = self.other(step)
+            self.copy(target.at[j], target.at[j], sems, j, j, j).wait_recv()
+
+    def sent(self, source, sems):
+        for step in range(1, 8):
+            j = self.other(step)
+            self.copy(source.at[j], source.at[j], sems, j, j, j).wait_send()
+
+
+def mask_columns(notes, neg):
+    for j in range(8):
+        neg[j * TOKENS : (j + 1) * TOKENS] = jnp.broadcast_to(notes[j, 0:1], (TOKENS, TOKENS)).T
+
+
+LEFTS = (WIDE, WIDE, WIDE, DEEP)
+RIGHTS = (3 * WIDE, WIDE, DEEP, WIDE)
+LEFT_AT = (0, WIDE, 2 * WIDE, 3 * WIDE)
+RIGHT_AT = (0, 3 * WIDE, 4 * WIDE, 4 * WIDE + DEEP)
+N_LEFT = 3 * WIDE + DEEP
+N_RIGHT = 5 * WIDE + DEEP
+
+
+def pools_of(block):
+    left = jnp.zeros_like(block)
+    right = jnp.zeros_like(block)
+    for at, base in enumerate((QKV_AT, OUT_AT, UP_AT, DOWN_AT)):
+        inside = block >= base
+        cols = RIGHTS[at]
+        left = jnp.where(inside, LEFT_AT[at] + (block - base) // cols, left)
+        right = jnp.where(inside, RIGHT_AT[at] + (block - base) % cols, right)
+    return left, right
+
+
+def halves(value):
+    high = value.astype(LOW)
+    return high, (value - high.astype(FULL)).astype(LOW)
+
+
+def fine(left, right):
+    return dot(
+        jnp.concatenate([left[0], left[1], left[0]], axis=1),
+        jnp.concatenate([right[0], right[0], right[1]], axis=0),
+    )
+
+
+def statistic(gram, shrink, diag, eye):
+    return jnp.where(eye, 0.5 * diag, 0.0) + shrink * gram
+
+
+def roots(stats, eye):
+    scales = [jnp.sqrt(jnp.sum(jnp.sum(stat * stat, axis=1, keepdims=True), axis=0, keepdims=True)) for stat in stats]
+    moving = [stat / scale for stat, scale in zip(stats, scales)]
+    approx = [None] * len(stats)
+    ahead = range(len(stats))
+    for iteration in range(ITERS):
+        factors = [(jnp.where(eye, 5.0, 0.0) - moving[i]) * 0.25 for i in ahead]
+        parts = [halves(factor) for factor in factors]
+        if iteration == 0:
+            approx = [factors[i] * lax.rsqrt(jnp.sqrt(scales[i])) for i in ahead]
+        else:
+            approx = [fine(halves(approx[i]), parts[i]) for i in ahead]
+        if iteration < ITERS - 1:
+            squares = [halves(fine(parts[i], parts[i])) for i in ahead]
+            fourths = [halves(fine(squares[i], squares[i])) for i in ahead]
+            moving = [fine(fourths[i], halves(moving[i])) for i in ahead]
+    return approx
+
+
+PAIRED = 2
+SUM_SCRATCH = (
+    ("left_t", pltpu.VMEM((N_LEFT, BS, 4 * TOKENS), LOW)),
+    ("right_pool", pltpu.VMEM((N_RIGHT, 4 * TOKENS, BS), LOW)),
+    ("x_stage", pltpu.VMEM((2, 2, 4, PAIRED, BS, BS), LOW)),
+    ("x_land", pltpu.VMEM((2, 2, 4, PAIRED, BS, BS), LOW)),
+    ("yb_stage", pltpu.VMEM((4, QUART, BS, BS), LOW)),
+    ("yb_land", pltpu.VMEM((4, QUART, BS, BS), LOW)),
+    ("ym_stage", pltpu.VMEM((2, 4, PAIRED, BS, BS), LOW)),
+    ("ym_land", pltpu.VMEM((2, 4, PAIRED, BS, BS), LOW)),
+    ("zb_stage", pltpu.VMEM((4, QUART, BS, BS), LOW)),
+    ("zb_land", pltpu.VMEM((3, QUART, BS, BS), LOW)),
+    ("zm_stage", pltpu.VMEM((2, 4, PAIRED, BS, BS), LOW)),
+    ("zm_land", pltpu.VMEM((2, 3, PAIRED, BS, BS), LOW)),
+    ("both_stage", pltpu.VMEM((2, PAIRED, BS, BS), LOW)),
+    ("both_land", pltpu.VMEM((PAIRED, BS, BS), LOW)),
+    ("own", pltpu.VMEM((6, BS, BS), LOW)),
+    ("staged", pltpu.VMEM((6, BS, BS), LOW)),
+    ("pair_rows", pltpu.VMEM((20, D), FULL)),
+    ("chip_rows", pltpu.VMEM((20, D), FULL)),
+    ("plane_rows", pltpu.VMEM((20, D), FULL)),
+    ("row_land", pltpu.VMEM((3, 20, D), FULL)),
+    ("row_z", pltpu.VMEM((4, 20, D), FULL)),
+    ("pool_sems", pltpu.SemaphoreType.DMA((2,))),
+    ("send_sems", pltpu.SemaphoreType.DMA((11, 4))),
+    ("recv_sems", pltpu.SemaphoreType.DMA((11, 4))),
+    ("row_send", pltpu.SemaphoreType.DMA((6,))),
+    ("row_recv", pltpu.SemaphoreType.DMA((6,))),
+    ("share_send", pltpu.SemaphoreType.DMA((6, 6))),
+    ("share_recv", pltpu.SemaphoreType.DMA((6, 6))),
+    ("local_sems", pltpu.SemaphoreType.DMA((9,))),
+    ("swap_local", pltpu.SemaphoreType.DMA((1,))),
+    ("swap_send", pltpu.SemaphoreType.DMA((1,))),
+    ("swap_recv", pltpu.SemaphoreType.DMA((1,))),
+)
+SUM_INPUTS = ("left_ids", "right_ids", "rows_in", "left_diag", "right_diag", "grad_in", "left_in", "right_in")
+SUM_OUTPUTS = ("rows_out", "grads_out", "moves_out", "grad_out")
+
+
+def update_kernel(*refs):
+    r = Refs()
+    for name, ref in zip(SUM_INPUTS + SUM_OUTPUTS + tuple(name for name, unused in SUM_SCRATCH), refs):
+        setattr(r, name, ref)
+    here = [
+        pltpu.make_async_copy(r.right_in, r.right_pool, r.pool_sems.at[0]),
+        pltpu.make_async_copy(r.left_in, r.left_t, r.pool_sems.at[1]),
+    ]
+    for copy in here:
+        copy.start()
+    x, c, z, y = place()
+    samp = 2 * x + c
+    blk = 2 * z + y
+    to_c = (2 * x + 1 - c, blk)
+    to_x = (2 * (1 - x) + c, blk)
+    to_y = (samp, 2 * z + 1 - y)
+    to_z = [(samp, 2 * lax.rem(z + step, 4) + y) for step in (1, 2, 3)]
+    meet_all()
+    swap = Swap(r.swap_local, r.swap_send, r.swap_recv)
+    swap.start(r.grad_in, r.grad_out)
+    row_copies = [push(r.rows_in, r.row_land.at[0], r.row_send.at[0], r.row_recv.at[0], to_c)]
+    eye = lax.broadcasted_iota(jnp.int32, (BS, BS), 0) == lax.broadcasted_iota(jnp.int32, (BS, BS), 1)
+
+    def group(half, k):
+        return 2 * lax.rem(z + 1 + k, 4) + (1 - y if half == 0 else y)
+
+    def part(half, k, offset, count=PAIRED):
+        slot = group(half, k) * GROUP + c * HALF + offset
+        return [dot(r.left_t[r.left_ids[slot + i]], r.right_pool[r.right_ids[slot + i]]) for i in range(count)]
+
+    def mine(batch):
+        return x * 8 + PAIRED * batch
+
+    def other(batch):
+        return (1 - x) * 8 + PAIRED * batch
+
+    both = QUART
+
+    def link(kind, k, stage, land, to):
+        return pltpu.make_async_remote_copy(
+            src_ref=stage, dst_ref=land, send_sem=r.send_sems.at[kind, k], recv_sem=r.recv_sems.at[kind, k],
+            device_id=to, device_id_type=MESH,
+        )
+
+    def along_x(batch, half, k):
+        return link(2 * batch + half, k, r.x_stage.at[batch, half, k], r.x_land.at[batch, half, k], to_x)
+
+    def along_y_both(k):
+        return link(4, k, r.yb_stage.at[k], r.yb_land.at[k], to_y)
+
+    def along_y(batch, k):
+        return link(5 + batch, k, r.ym_stage.at[batch, k], r.ym_land.at[batch, k], to_y)
+
+    def along_z_both(k):
+        return link(7, k, r.zb_stage.at[k], r.zb_land.at[k], (samp, group(1, k)))
+
+    def along_z(batch, k):
+        return link(8 + batch, k, r.zm_stage.at[batch, k], r.zm_land.at[batch, k], (samp, group(1, k)))
+
+    def last():
+        return link(10, 0, r.both_stage.at[1 - x], r.both_land, to_x)
+
+    def send_x(batch, half, k):
+        for i, value in enumerate(part(half, k, other(batch))):
+            r.x_stage[batch, half, k, i] = value.astype(LOW)
+        along_x(batch, half, k).start()
+
+    def add_x_send_y(batch, k):
+        values = part(0, k, mine(batch))
+        along_x(batch, 0, k).wait_recv()
+        for i, value in enumerate(values):
+            r.ym_stage[batch, k, i] = (value + r.x_land[batch, 0, k, i].astype(FULL)).astype(LOW)
+        along_y(batch, k).start()
+
+    def add_both_send_z(batch, k):
+        values = part(1, k, mine(batch))
+        along_x(batch, 1, k).wait_recv()
+        values = [value + r.x_land[batch, 1, k, i].astype(FULL) for i, value in enumerate(values)]
+        along_y(batch, k).wait_recv()
+        for i, value in enumerate(values):
+            r.zm_stage[batch, k, i] = (value + r.ym_land[batch, k, i].astype(FULL)).astype(LOW)
+
+        @pl.when(k < 3)
+        def send_on():
+            along_z(batch, k).start()
+
+    def each(step):
+        def body(k, carry):
+            step(k)
+            return carry
+
+        lax.fori_loop(0, 4, body, 0)
+
+    def slot_of(i, far=False):
+        side = (1 - x) if far else x
+        return c * HALF + (side * 8 + i if i < QUART else QUART + 2 * side + i - QUART)
+
+    def share(kind, k, src, dst, to):
+        return pltpu.make_async_remote_copy(
+            src_ref=src, dst_ref=dst, send_sem=r.share_send.at[kind, k], recv_sem=r.share_recv.at[kind, k],
+            device_id=to, device_id_type=MESH,
+        )
+
+    def grad_to(kind, pair, to):
+        place_out = r.grads_out.at[pl.ds(slot_of(PAIRED * pair), PAIRED)]
+        return share(kind, pair, r.own.at[pl.ds(PAIRED * pair, PAIRED)], place_out, to)
+
+    def grad_on(pair):
+        place_out = r.grads_out.at[pl.ds(slot_of(PAIRED * pair, True), PAIRED)]
+        return share(2, pair, place_out, place_out, to_c)
+
+    def grad_kept(pair):
+        place_out = r.grads_out.at[pl.ds(slot_of(PAIRED * pair), PAIRED)]
+        return pltpu.make_async_copy(r.own.at[pl.ds(PAIRED * pair, PAIRED)], place_out, r.local_sems.at[6 + pair])
+
+    def move_to(kind, i, to):
+        return share(kind, i, r.staged.at[i], r.moves_out.at[slot_of(i)], to)
+
+    def move_on(i):
+        place_out = r.moves_out.at[slot_of(i, True)]
+        return share(5, i, place_out, place_out, to_c)
+
+    def move_kept(i):
+        return pltpu.make_async_copy(r.staged.at[i], r.moves_out.at[slot_of(i)], r.local_sems.at[i])
+
+    def share_grads(pair):
+        grad_to(0, pair, to_x).start()
+        grad_to(1, pair, to_c).start()
+        grad_kept(pair).start()
+
+    def directions(pair):
+        held = []
+        stats = []
+        for i in range(PAIRED * pair, PAIRED * pair + PAIRED):
+            low = r.own[i]
+            grad = low.astype(FULL)
+            mean = jnp.sum(jnp.sum(grad * grad, axis=1, keepdims=True), axis=0, keepdims=True) / (BS * BS)
+            shrink = 0.5 / (mean + 1e-06)
+            low_t = grad.T.astype(LOW)
+            slot = slot_of(i)
+            stats.append(statistic(dot(low, low_t), shrink, r.left_diag[pl.ds(slot, 1)], eye))
+            stats.append(statistic(dot(low_t, low), shrink, r.right_diag[pl.ds(slot, 1)], eye))
+            held.append((i, low, lax.rsqrt(mean + 1e-06)))
+        sides = roots(stats, eye)
+        for n, (i, low, rate) in enumerate(held):
+            high, rest = halves(sides[2 * n])
+            turned = dot(jnp.concatenate([high, rest], axis=1), jnp.concatenate([low, low], axis=0)) * rate
+            r.staged[i] = fine(halves(turned), halves(sides[2 * n + 1])).astype(LOW)
+            move_to(3, i, to_x).start()
+            move_to(4, i, to_c).start()
+            move_kept(i).start()
+
+    def finish_batch(batch):
+        for k in range(3):
+            along_z(batch, k).wait_recv()
+        for i in range(PAIRED):
+            value = r.zm_stage[batch, 3, i].astype(FULL)
+            for k in range(3):
+                value = value + r.zm_land[batch, k, i].astype(FULL)
+            r.own[PAIRED * batch + i] = value.astype(LOW)
+        share_grads(batch)
+
+    def pass_on(pair):
+        grad_to(0, pair, to_x).wait_recv()
+        grad_on(pair).start()
+        for i in range(PAIRED * pair, PAIRED * pair + PAIRED):
+            move_to(3, i, to_x).wait_recv()
+            move_on(i).start()
+
+    for copy in here:
+        copy.wait()
+
+    @each
+    def begin(k):
+        for i, value in enumerate(part(0, k, both, QUART)):
+            r.yb_stage[k, i] = value.astype(LOW)
+        along_y_both(k).start()
+        send_x(0, 0, k)
+
+    @each
+    def more(k):
+        send_x(0, 1, k)
+
+    row_copies[0].wait_recv()
+    r.pair_rows[...] = r.rows_in[...] + r.row_land[0]
+    row_copies.append(push(r.pair_rows, r.row_land.at[1], r.row_send.at[1], r.row_recv.at[1], to_x))
+
+    @each
+    def middle(k):
+        add_x_send_y(0, k)
+        values = part(1, k, both, QUART)
+        along_y_both(k).wait_recv()
+        for i, value in enumerate(values):
+            r.zb_stage[k, i] = (value + r.yb_land[k, i].astype(FULL)).astype(LOW)
+
+        @pl.when(k < 3)
+        def send_on():
+            along_z_both(k).start()
+
+        send_x(1, 0, k)
+
+    row_copies[1].wait_recv()
+    r.chip_rows[...] = r.pair_rows[...] + r.row_land[1]
+    row_copies.append(push(r.chip_rows, r.row_land.at[2], r.row_send.at[2], r.row_recv.at[2], to_y))
+
+    @each
+    def late(k):
+        add_both_send_z(0, k)
+
+    for k in range(3):
+        along_z_both(k).wait_recv()
+    for i in range(QUART):
+        value = r.zb_stage[3, i].astype(FULL)
+        for k in range(3):
+            value = value + r.zb_land[k, i].astype(FULL)
+        r.both_stage[i // 2, i % 2] = value.astype(LOW)
+    last().start()
+
+    @each
+    def more_again(k):
+        send_x(1, 1, k)
+
+    @each
+    def middle_again(k):
+        add_x_send_y(1, k)
+
+    row_copies[2].wait_recv()
+    r.plane_rows[...] = r.chip_rows[...] + r.row_land[2]
+    for step in range(3):
+        row_copies.append(
+            push(r.plane_rows, r.row_z.at[z], r.row_send.at[3 + step], r.row_recv.at[3 + step], to_z[step])
+        )
+    r.row_z[z] = r.plane_rows[...]
+    last().wait_recv()
+    for i in range(PAIRED):
+        r.own[QUART + i] = (r.both_stage[x, i].astype(FULL) + r.both_land[i].astype(FULL)).astype(LOW)
+    share_grads(2)
+    directions(2)
+
+    @each
+    def late_again(k):
+        add_both_send_z(1, k)
+
+    finish_batch(0)
+    directions(0)
+    for step in range(3):
+        row_copies[3 + step].wait_recv()
+    r.rows_out[...] = (r.row_z[0] + r.row_z[1]) + (r.row_z[2] + r.row_z[3])
+    finish_batch(1)
+    pass_on(2)
+    directions(1)
+    pass_on(0)
+    pass_on(1)
+    for pair in range(3):
+        grad_to(1, pair, to_c).wait_recv()
+        grad_on(pair).wait_recv()
+        grad_to(0, pair, to_x).wait_send()
+        grad_to(1, pair, to_c).wait_send()
+        grad_on(pair).wait_send()
+        grad_kept(pair).wait()
+    for i in range(6):
+        move_to(4, i, to_c).wait_recv()
+        move_on(i).wait_recv()
+        move_to(3, i, to_x).wait_send()
+        move_to(4, i, to_c).wait_send()
+        move_on(i).wait_send()
+        move_kept(i).wait()
+    for copy in row_copies:
+        copy.wait_send()
+    last().wait_send()
+
+    @each
+    def drain(k):
+        along_y_both(k).wait_send()
+        for batch in range(2):
+            along_x(batch, 0, k).wait_send()
+            along_x(batch, 1, k).wait_send()
+            along_y(batch, k).wait_send()
+
+        @pl.when(k < 3)
+        def sent_on():
+            along_z_both(k).wait_send()
+            for batch in range(2):
+                along_z(batch, k).wait_send()
+
+    swap.finish()
+
+
+def update(left_ids, right_ids, rows, left_start, right_start, grad, left_pool, right_pool):
+    return pl.pallas_call(
+        update_kernel,
+        out_shape=(SHAPES["rows"], shape((GROUP, BS, BS)), shape((GROUP, BS, BS)), SHAPES["pred"]),
+        in_specs=[SMEM_IN] * 2 + [VMEM_AT] * 3 + [ANY_AT] * 3,
+        out_specs=(VMEM_AT,) + (ANY_AT,) * 3,
+        scratch_shapes=[spec for unused, spec in SUM_SCRATCH],
+        compiler_params=pltpu.CompilerParams(
+            collective_id=1, has_side_effects=True, vmem_limit_bytes=VMEM_ASK
+        ),
+        cost_estimate=pl.CostEstimate(flops=36 << 30, bytes_accessed=40 << 20, transcendentals=0),
+        name="update",
+    )(left_ids, right_ids, rows, left_start, right_start, grad, left_pool, right_pool)
+
+
+def finish_kernel(grad, move, weight, left_diag, right_diag, grad_out, left_out, right_out, new_out, low_out):
+    eye = lax.broadcasted_iota(jnp.int32, (BS, BS), 0) == lax.broadcasted_iota(jnp.int32, (BS, BS), 1)
+
+    def mean(value):
+        return jnp.sum(jnp.sum(value, axis=1, keepdims=True), axis=0, keepdims=True) / (BS * BS)
+
+    for i in range(STEP):
+        low = grad[i]
+        full = low.astype(FULL)
+        grad_out[i] = full
+        shrink = 0.5 / (mean(full * full) + 1e-06)
+        low_t = full.T.astype(LOW)
+        left_out[i] = statistic(dot(low, low_t), shrink, left_diag[i], eye)
+        right_out[i] = statistic(dot(low_t, low), shrink, right_diag[i], eye)
+        step = move[i].astype(FULL)
+        start = weight[i]
+        ratio = jnp.sqrt(mean(start * start)) * lax.rsqrt(mean(step * step) + 1e-06)
+        new = start - step_rate * ratio * step
+        new_out[i] = new
+        low_out[i] = new.astype(LOW)
+
+
+STEP = 4
+
+
+def finish_slots(grads, moves, masters, left_start, right_start):
+    block = pl.BlockSpec((STEP, BS, BS), lambda i: (i, 0, 0))
+    row = pl.BlockSpec((STEP, 1, BS), lambda i: (i, 0, 0))
+    return pl.pallas_call(
+        finish_kernel,
+        grid=(GROUP // STEP,),
+        compiler_params=pltpu.CompilerParams(vmem_limit_bytes=VMEM_ASK),
+        out_shape=tuple(shape((GROUP, BS, BS), kind) for kind in (FULL, FULL, FULL, FULL, LOW)),
+        in_specs=[block, block, block, row, row],
+        out_specs=(block,) * 5,
+        cost_estimate=pl.CostEstimate(flops=2 << 30, bytes_accessed=39 << 20, transcendentals=0),
+        name="finish_slots",
+    )(grads, moves, masters, left_start.reshape(GROUP, 1, BS), right_start.reshape(GROUP, 1, BS))
+
+
+def local_tuned(
+    inputs,
+    cot_first,
+    cot_second,
+    valid_flags,
+    lead_steps,
+    masters,
+    assignment,
+    left_start,
+    right_start,
+    vectors,
+    vec_moment,
+):
+    notes = jnp.concatenate(
+        [
+            valid_flags.astype(FULL) - 1.0,
+            jnp.pad(lead_steps.astype(FULL).T, ((0, 0), (0, TOKENS - 2))),
+            jnp.zeros((6, TOKENS), FULL),
+        ],
+        axis=0,
+    )
+    left_pool, right_pool, pred_one, pred_two, input_grad, rows = model(
+        assignment, masters, notes, inputs, cot_first, cot_second, vectors
+    )
+    position = jnp.arange(NB, dtype=jnp.int32)
+    inverse = jnp.sum(
+        jnp.where(assignment[None, :] == position[:, None], position[None, :], 0), axis=1
+    )
+    left_ids, right_ids = pools_of(inverse)
+    vec_grads, grads, moves, input_grad = update(
+        left_ids, right_ids, rows, left_start, right_start, input_grad, left_pool, right_pool
+    )
+    input_grad = input_grad.astype(FULL)
+    matrix_grads, left_stats, right_stats, new_masters, new_copies = finish_slots(
+        grads, moves, masters, left_start, right_start
+    )
+    scaled_vec = vec_grads * lax.rsqrt(
+        jnp.mean(vec_grads * vec_grads, axis=1, keepdims=True) + 1e-06
+    )
+    vec_moments = 0.5 * vec_moment + 0.5 * scaled_vec * scaled_vec
+    new_vectors = vectors - vector_rate * scaled_vec * lax.rsqrt(vec_moments)
+    return (
+        pred_one,
+        pred_two,
+        input_grad,
+        matrix_grads,
+        left_stats,
+        right_stats,
+        new_masters,
+        new_copies,
+        vec_grads,
+        vec_moments,
+        new_vectors,
+    )
+
+
 def solution(mesh):
     placed = (
         P("samp", "blk", None),
@@ -480,8 +1887,9 @@
         P(),
         P(),
     )
+    fits = mesh.shape["samp"] == 4 and mesh.shape["blk"] == 8
     return jax.shard_map(
-        local,
+        local_tuned if fits else local_any,
         mesh=mesh,
         in_specs=placed,
         out_specs=(

time: 2780 us -> 412 us (0.15)
  waiting for transfers between devices: 1560 us -> 0 us
  matrix products: 619 us -> 0 us
  Pallas kernels: 0 us -> 395 us
  local copies, waits for them, and re-layouts: 316 us -> 3.41 us
  other arithmetic: 134 us -> 4.42 us
  blocking collectives: 117 us -> 0 us
    reduce_scatter x1 -> x0, waiting for transfers between devices: 799 us -> none  [local(): shared = lax.psum_scatter(slotted, 'blk', scatter_dimension=0, tiled=True)]
    dot_general x84 -> x0, matrix products: 619 us -> none  [the longest x12 128 us: invert_root(): approx = jnp.dot(approx, factor, precision=HIGH)]
    all_gather x9 -> x0, waiting for transfers between devices: 583 us -> none  [the longest x1 479 us: local(): lax.all_gather(masters.astype(jnp.bfloat16), 'blk', axis=0, tiled=True)]
    pallas_call x0 -> x3, Pallas kernels: none -> 395 us  [the longest x1 232 us: model(): pl.pallas_call(model_kernel, out_shape=(shape((N_LEFT, BS, 4 * TOKENS)),...]
    psum x2 -> x0, waiting for transfers between devices: 180 us -> none  [the longest x1 111 us: local(): vec_grads = lax.psum(vec_one + vec_two, ('samp', 'blk'))]
    all_gather x5 -> x0, blocking collectives: 117 us -> none  [the longest x2 50.7 us: backward(): lax.all_gather(inner, 'blk', axis=1, tiled=True)]
    reshape x14 -> x2, local copies, waits for them, and re-layouts: 115 us -> 1.25 us  [the longest x1 0.63 us: finish_slots(): left_start.reshape(GROUP, 1, BS)]
    select_n x4 -> x1, other arithmetic: 55.5 us -> 0.59 us  [pools_of(): right = jnp.where(inside, RIGHT_AT[at] + (block - base) % cols, right)]
  transfers between devices with their start and end apart: 12 -> 0, of which waited for: 9 -> 0; matrix products, arithmetic and copies ran while one was open for 11% -> 0% of each run, Pallas kernels for 0% -> 0%
where the time goes in v2:
time: 412 us; the launch traced here: 404 us
  Pallas kernels  395 us (96%)
  other arithmetic  4.42 us (1%)
    pallas_call x1, Pallas kernels, model(): pl.pallas_call(model_kernel, out_shape=(shape((N_LEFT, BS, 4 * TOKENS)),...  232 us
    pallas_call x1, Pallas kernels, update(): pl.pallas_call(update_kernel, out_shape=(SHAPES['rows'], shape((GROUP, BS...  148 us
    pallas_call x1, Pallas kernels, finish_slots(): pl.pallas_call(finish_kernel, grid=(GROUP // STEP,), compiler_params=pltp...  15.1 us

profile of v2, /device:TPU:3, one launch (start us, length us, event | category | flops | bytes accessed | tf_op | source)
XLA Modules:
  0.0 404.3 jit_solution(15178907706377281039)
XLA Ops:
  0.7 0.1 pad.7.clone
  0.7 0.7 convert_add_fusion
  1.4 0.7 convert_bitcast_fusion
  2.0 0.7 fusion.1.refs_2_
  2.7 0.0 copy-start.8
  2.7 232.3 %model.1 = (bf16[28,256,512]{2,1,0:T(8,128)(2,1)}, bf16[36,512,256]{2,1,0:T(8,128)(2,1)}, bf16[1,128,1024]{2,1,0:T(8,128)(2,1)}, bf16[1,128,1024]{2,1,0:T(8,128)...) custom-call(s32[192]{0:T(256)} %refs_0_.1, f32[24,256,256]{2,1,0:T(8,128)} %weight.1, f32[8,128]{1,0:T(8,128)} %fusion.1.refs_2_, ...), custom_call_target="tpu_custom_call" | custom-call | flops 25769803776 | bytes 62914560 | tf_op jit(solution)/shard_map/model/pallas_call | solution.py:1275
  235.0 0.0 copy-done.8
  235.0 0.1 select_reduce_fusion
  235.1 0.6 fusion.4
  235.7 0.0 copy-start.7
  235.7 147.8 %update.1 = (f32[20,1024]{1,0:T(8,128)}, bf16[24,256,256]{2,1,0:T(8,128)(2,1)}, bf16[24,256,256]{2,1,0:T(8,128)(2,1)}, bf16[1,128,1024]{2,1,0:T(8,128)(2,1)}) custom-call(s32[192]{0:T(256)} %get-tuple-element.44.refs_0_, s32[192]{0:T(256)} %get-tuple-element.43.refs_1_, f32[20,1024]{1,0:T(8,128)} %get-tuple-element.28.refs_2_, f32[24,256]{1,0:T(8,128)} %refs_3_.3, ...), custom_call_target="tpu_custom_call" | custom-call | flops 38654705664 | bytes 41943040 | tf_op jit(solution)/shard_map/update/pallas_call | solution.py:1766
  383.6 0.0 copy-done.6
  383.6 0.6 reshape.37.left_diag
  384.2 0.0 copy-done.7
  384.2 0.6 reshape.38.right_diag
  384.8 0.0 copy-start
  384.8 0.0 copy-start.4
  384.8 0.0 copy-start.3
  384.9 0.0 copy-start.2
  384.9 15.1 %finish_slots.1 = (f32[24,256,256]{2,1,0:T(8,128)}, f32[24,256,256]{2,1,0:T(8,128)}, f32[24,256,256]{2,1,0:T(8,128)}, f32[24,256,256]{2,1,0:T(8,128)}, bf16[24,256,256]{2,1,0:T(8,128)(2,1)}) custom-call(bf16[24,256,256]{2,1,0:T(8,128)(2,1)} %get-tuple-element.33.grad, bf16[24,256,256]{2,1,0:T(8,128)(2,1)} %get-tuple-element.34.move, f32[24,256,256]{2,1,0:T(8,128)} %weight.1, ...), custom_call_target="tpu_custom_call" | custom-call | flops 2147483648 | bytes 40894464 | tf_op jit(solution)/shard_map/finish_slots/pallas_call | solution.py:1808
  400.0 0.0 copy-done
  400.0 0.1 multiply_reduce_fusion
  400.1 0.0 copy-done.4
  400.1 0.0 copy-done.5
  400.2 0.8 multiply_subtract_fusion
  400.9 0.0 copy-done.1
  400.9 0.8 convert_element_type.13
  401.8 0.0 copy-done.3
  401.8 0.7 copy.25
  402.5 0.0 copy-done.2
  402.5 0.7 copy.26
  403.2 0.6 copy.27
  (5 shorter events, 0.0 us)
Async XLA Ops:
  2.7 232.3 %copy-start.8 = (s32[192]{0:T(256)S(1)}, s32[192]{0:T(256)}, u32[]{:S(2)}) copy-start(s32[192]{0:T(256)} %refs_0_.1) | copy-start | bytes 2308
  235.7 147.8 %copy-start.6 = (f32[24,256]{1,0:T(8,128)S(1)}, f32[24,256]{1,0:T(8,128)}, u32[]{:S(2)}) copy-start(f32[24,256]{1,0:T(8,128)} %refs_3_.3) | copy-start | bytes 73732
  235.7 148.5 %copy-start.7 = (f32[24,256]{1,0:T(8,128)S(1)}, f32[24,256]{1,0:T(8,128)}, u32[]{:S(2)}) copy-start(f32[24,256]{1,0:T(8,128)} %refs_4_.3) | copy-start | bytes 73732
  384.8 15.2 %copy-start = (f32[20,1024]{1,0:T(8,128)S(1)}, f32[20,1024]{1,0:T(8,128)}, u32[]{:S(2)}) copy-start(f32[20,1024]{1,0:T(8,128)} %get-tuple-element.64) | copy-start | bytes 245764
  384.8 15.3 %copy-start.4 = (f32[20,1024]{1,0:T(8,128)S(1)}, f32[20,1024]{1,0:T(8,128)}, u32[]{:S(2)}) copy-start(f32[20,1024]{1,0:T(8,128)} %refs_6_.1) | copy-start | bytes 245764
  384.8 15.3 %copy-start.5 = (f32[20,1024]{1,0:T(8,128)S(1)}, f32[20,1024]{1,0:T(8,128)}, u32[]{:S(2)}) copy-start(f32[20,1024]{1,0:T(8,128)} %param.21) | copy-start | bytes 245764
  384.8 16.1 %copy-start.1 = (bf16[1,128,1024]{2,1,0:T(8,128)(2,1)S(1)}, bf16[1,128,1024]{2,1,0:T(8,128)(2,1)}, u32[]{:S(2)}) copy-start(bf16[1,128,1024]{2,1,0:T(8,128)(2,1)} %get-tuple-element.32) | copy-start | bytes 786436
  384.8 16.9 %copy-start.3 = (bf16[1,128,1024]{2,1,0:T(8,128)(2,1)S(1)}, bf16[1,128,1024]{2,1,0:T(8,128)(2,1)}, u32[]{:S(2)}) copy-start(bf16[1,128,1024]{2,1,0:T(8,128)(2,1)} %get-tuple-element.56) | copy-start | bytes 786436
  384.9 17.6 %copy-start.2 = (bf16[1,128,1024]{2,1,0:T(8,128)(2,1)S(1)}, bf16[1,128,1024]{2,1,0:T(8,128)(2,1)}, u32[]{:S(2)}) copy-start(bf16[1,128,1024]{2,1,0:T(8,128)(2,1)} %get-tuple-element.57) | copy-start | bytes 786436
